TPU v7x, 32 devices: a whole 2x2x4 slice. The times are simulated.
32 devices in a mesh: member: 8 (over y, x, core), space: 4 (over z).
Axes of the slice: x: 2, y: 2, z: 4, core: 2. Of those that a mesh axis runs over, the one named last changes fastest.
Arguments:
- layer_input: bfloat16 [32, 1024, 256], P('member', 'space'), may hold values from -6 to 6
- out_grad: bfloat16 [32, 1024, 256], P('member', 'space'), may hold values from -6 to 6
- norm1_gain: float32 [256], replicated, as said below
- w_query: bfloat16 [256, 256], replicated, as said below
- w_key: bfloat16 [256, 256], replicated, as said below
- w_value: bfloat16 [256, 256], replicated, may hold values from -0.375 to 0.375
- w_out: bfloat16 [256, 256], replicated, may hold values from -0.375 to 0.375
- norm2_gain: float32 [256], replicated, may hold values from 0.5 to 1.5
- w_up: bfloat16 [256, 1024], replicated, may hold values from -0.375 to 0.375
- w_down: bfloat16 [1024, 256], replicated, may hold values from -0.1875 to 0.1875
Outputs:
- input_grad: float32 [32, 1024, 256], P('member', 'space')
- grad_query: float32 [256, 256], replicated
- grad_key: float32 [256, 256], replicated
- grad_value: float32 [256, 256], replicated
- grad_wout: float32 [256, 256], replicated
- grad_up: float32 [256, 1024], replicated
- grad_down: float32 [1024, 256], replicated
- grad_gain1: float32 [256], replicated
- grad_gain2: float32 [256], replicated
Inputs may be any that keep to these rules, and one draw needn't show every extreme that they name: `norm1_gain`: positive gains, between 0.5 and 3. `w_query`: entries of a query projection. `w_key`: entries of a key projection.
All inputs are finite; a program needn't handle non-finite values.
Results may differ from a plain program's by a relative error of at most 0.008.
The roundings to bfloat16 on the way count: a program that leaves them out, or rounds other values in their place, can miss the bound.
Values may be sent and summed in bfloat16 or wider, within the bound.
A program may use at most 128 MiB of HBM per device.

v0:
```python
import math

import jax
import jax.numpy as jnp
from jax import lax
from jax.sharding import PartitionSpec as P

HEAD_DIM = 32


EPS = 1e-06
GELU_C = 0.7978845608028654
GELU_A = 0.044715


def multiply(form, left, right):
    return jnp.einsum(form, left, right, preferred_element_type=jnp.float32)


def norm_rows(values):
    inverse = lax.rsqrt(jnp.mean(values * values, axis=-1, keepdims=True) + EPS)
    return (values * inverse, inverse)


def norm_back(unit_rows, inverse, gains, upstream):
    scaled = upstream * gains
    into = inverse * (scaled - unit_rows * jnp.mean(scaled * unit_rows, axis=-1, keepdims=True))
    return (into, jnp.sum(upstream * unit_rows, axis=(0, 1)))


def gelu_pair(preact):
    tangent = jnp.tanh(GELU_C * (preact + GELU_A * preact * preact * preact))
    result = 0.5 * preact * (1.0 + tangent)
    slopes = 0.5 * (1.0 + tangent) + 0.5 * preact * (1.0 - tangent * tangent) * GELU_C * (
        1.0 + 3.0 * GELU_A * preact * preact
    )
    return (result, slopes)


def attend(query, keys, values, heads):
    members, count, width = query.shape
    shape_four = (members, count, heads, width // heads)
    scale = 1.0 / math.sqrt(width // heads)
    scores = (
        multiply("mphe,nphe->phmn", query.reshape(shape_four), keys.reshape(shape_four)) * scale
    )
    scores = scores - jnp.max(scores, axis=-1, keepdims=True)
    weights = jnp.exp(scores)
    weights = weights / jnp.sum(weights, axis=-1, keepdims=True)
    rounded = weights.astype(jnp.bfloat16)
    mixed = multiply("phmn,nphe->mphe", rounded, values.reshape(shape_four)).astype(jnp.bfloat16)
    return (weights, rounded, mixed.reshape(members, count, width))


def attend_back(query, keys, values, weights, rounded, upstream, heads):
    members, count, width = query.shape
    shape_four = (members, count, heads, width // heads)
    scale = 1.0 / math.sqrt(width // heads)
    up_four = upstream.reshape(shape_four)
    dprob = multiply("mphe,nphe->phmn", up_four, values.reshape(shape_four))
    grad_v = multiply("phmn,mphe->nphe", rounded, up_four).astype(jnp.bfloat16)
    dscore = (weights * (dprob - jnp.sum(weights * dprob, axis=-1, keepdims=True)) * scale).astype(
        jnp.bfloat16
    )
    grad_q = multiply("phmn,nphe->mphe", dscore, keys.reshape(shape_four)).astype(jnp.bfloat16)
    grad_k = multiply("phmn,mphe->nphe", dscore, query.reshape(shape_four)).astype(jnp.bfloat16)
    return (
        grad_q.reshape(members, count, width),
        grad_k.reshape(members, count, width),
        grad_v.reshape(members, count, width),
    )


def on_device(
    layer_input, out_grad, norm1_gain, w_query, w_key, w_value, w_out, norm2_gain, w_up, w_down
):
    groups = lax.axis_size("member")
    own_members, own_patches, width = layer_input.shape
    spread = own_patches // groups
    everyone = own_members * groups
    heads = width // HEAD_DIM

    def patchwise(array):
        return array.reshape(own_members, groups, spread, array.shape[-1])

    def memberwise(array):
        return array.reshape(everyone, 1, spread, array.shape[-1])

    wide = layer_input.astype(jnp.float32)
    unit1, inverse1 = norm_rows(wide)
    normed1 = (unit1 * norm1_gain).astype(jnp.bfloat16)
    query = multiply("mpd,de->mpe", normed1, w_query).astype(jnp.bfloat16)
    keys = multiply("mpd,de->mpe", normed1, w_key).astype(jnp.bfloat16)
    values = multiply("mpd,de->mpe", normed1, w_value).astype(jnp.bfloat16)
    moved = (
        lax.all_to_all(patchwise(query), "member", split_axis=1, concat_axis=0, tiled=True),
        lax.all_to_all(patchwise(keys), "member", split_axis=1, concat_axis=0, tiled=True),
        lax.all_to_all(patchwise(values), "member", split_axis=1, concat_axis=0, tiled=True),
    )
    query_here = moved[0].reshape(everyone, spread, width)
    keys_here = moved[1].reshape(everyone, spread, width)
    values_here = moved[2].reshape(everyone, spread, width)
    weights, rounded, mixed_here = attend(query_here, keys_here, values_here, heads)
    mixed = lax.all_to_all(
        memberwise(mixed_here), "member", split_axis=0, concat_axis=1, tiled=True
    ).reshape(own_members, own_patches, width)
    hidden_state = wide + multiply("mpd,de->mpe", mixed, w_out)
    unit2, inverse2 = norm_rows(hidden_state)
    normed2 = (unit2 * norm2_gain).astype(jnp.bfloat16)
    preact = multiply("mpd,df->mpf", normed2, w_up)
    activated, slopes = gelu_pair(preact)
    activated = activated.astype(jnp.bfloat16)
    part_down = multiply("mpf,mpd->fd", activated, out_grad)
    grad_act = multiply("mpd,fd->mpf", out_grad, w_down)
    grad_pre = (grad_act * slopes).astype(jnp.bfloat16)
    part_up = multiply("mpd,mpf->df", normed2, grad_pre)
    grad_normed2 = multiply("mpf,df->mpd", grad_pre, w_up)
    back_two, part_gain2 = norm_back(unit2, inverse2, norm2_gain, grad_normed2)
    grad_hidden = out_grad.astype(jnp.float32) + back_two
    grad_attn = grad_hidden.astype(jnp.bfloat16)
    part_wout = multiply("mpd,mpe->de", mixed, grad_attn)
    grad_mixed = multiply("mpe,de->mpd", grad_attn, w_out).astype(jnp.bfloat16)
    grad_mixed_here = lax.all_to_all(
        patchwise(grad_mixed), "member", split_axis=1, concat_axis=0, tiled=True
    ).reshape(everyone, spread, width)
    grad_q, grad_k, grad_v = attend_back(
        query_here, keys_here, values_here, weights, rounded, grad_mixed_here, heads
    )
    moved_back = (
        lax.all_to_all(memberwise(grad_q), "member", split_axis=0, concat_axis=1, tiled=True),
        lax.all_to_all(memberwise(grad_k), "member", split_axis=0, concat_axis=1, tiled=True),
        lax.all_to_all(memberwise(grad_v), "member", split_axis=0, concat_axis=1, tiled=True),
    )
    grad_q = moved_back[0].reshape(own_members, own_patches, width)
    grad_k = moved_back[1].reshape(own_members, own_patches, width)
    grad_v = moved_back[2].reshape(own_members, own_patches, width)
    part_query = multiply("mpd,mpe->de", normed1, grad_q)
    part_key = multiply("mpd,mpe->de", normed1, grad_k)
    part_value = multiply("mpd,mpe->de", normed1, grad_v)
    grad_normed1 = (
        multiply("mpe,de->mpd", grad_q, w_query)
        + multiply("mpe,de->mpd", grad_k, w_key)
        + multiply("mpe,de->mpd", grad_v, w_value)
    )
    back_one, part_gain1 = norm_back(unit1, inverse1, norm1_gain, grad_normed1)
    input_grad = grad_hidden + back_one
    totals = lax.psum(
        (part_query, part_key, part_value, part_wout, part_up, part_down, part_gain1, part_gain2),
        ("member", "space"),
    )
    scale = 1.0 / math.sqrt(everyone * own_patches * lax.axis_size("space"))
    return (
        input_grad,
        totals[0] * scale,
        totals[1] * scale,
        totals[2] * scale,
        totals[3] * scale,
        totals[4] * scale,
        totals[5] * scale,
        totals[6] * scale,
        totals[7] * scale,
    )


def solution(mesh):
    in_specs = (
        P("member", "space", None),
        P("member", "space", None),
        P(),
        P(),
        P(),
        P(),
        P(),
        P(),
        P(),
        P(),
    )
    out_specs = (P("member", "space", None), P(), P(), P(), P(), P(), P(), P(), P())
    return jax.shard_map(
        on_device, mesh=mesh, in_specs=in_specs, out_specs=out_specs, check_vma=False
    )
```

profile of v0, /device:TPU:0, one launch (start us, length us, event | category | flops | bytes accessed | tf_op | source)
XLA Modules:
  0.0 333.2 jit_solution(14394536945824989101)
XLA Ops:
  10.9 5.2 %all-to-all-start.1 = ((bf16[4,8,32,256]{3,2,0,1:T(8,128)(2,1)}), bf16[4,8,32,256]{3,2,0,1:T(8,128)(2,1)S(1)}, u32[]{:S(2)}, u32[]{:S(2)}) async-start(bf16[4,8,32,256]{3,2,0,1:T(8,128)(2,1)} %copy.95), calls=%async_computation.1 | async-start | bytes 1048576 | tf_op jit(solution)/shard_map/all_to_all | solution.py:96
  17.3 8.5 %all-to-all-done.1 = bf16[4,8,32,256]{3,2,0,1:T(8,128)(2,1)S(1)} async-done(((bf16[4,8,32,256]{3,2,0,1:T(8,128)(2,1)}), bf16[4,8,32,256]{3,2,0,1:T(8,128)(2,1)S(1)}, u32[]{:S(2)}, u32[]{:S(2)}) %all-to-all-start.1) | async-done | bytes 524320 | tf_op jit(solution)/shard_map/all_to_all | solution.py:96
  25.8 3.5 %all-to-all-start = ((bf16[4,8,32,256]{3,2,0,1:T(8,128)(2,1)}), bf16[4,8,32,256]{3,2,0,1:T(8,128)(2,1)S(1)}, u32[]{:S(2)}, u32[]{:S(2)}) async-start(bf16[4,8,32,256]{3,2,0,1:T(8,128)(2,1)} %copy.93), calls=%async_computation | async-start | bytes 1048576 | tf_op jit(solution)/shard_map/all_to_all | solution.py:98
  30.6 8.4 %all-to-all-done = bf16[4,8,32,256]{3,2,0,1:T(8,128)(2,1)S(1)} async-done(((bf16[4,8,32,256]{3,2,0,1:T(8,128)(2,1)}), bf16[4,8,32,256]{3,2,0,1:T(8,128)(2,1)S(1)}, u32[]{:S(2)}, u32[]{:S(2)}) %all-to-all-start) | async-done | bytes 524320 | tf_op jit(solution)/shard_map/all_to_all | solution.py:98
  39.0 4.2 %all-to-all-start.2 = ((bf16[4,8,32,256]{3,2,0,1:T(8,128)(2,1)}), bf16[4,8,32,256]{3,2,0,1:T(8,128)(2,1)}, u32[]{:S(2)}, u32[]{:S(2)}) async-start(bf16[4,8,32,256]{3,2,0,1:T(8,128)(2,1)} %copy.97), calls=%async_computation.2 | async-start | bytes 1048576 | tf_op jit(solution)/shard_map/all_to_all | solution.py:97
  58.3 6.3 %fusion.79 = (f32[32,8,32]{2,1,0:T(8,128)S(1)}, f32[32,8,32,32]{2,3,1,0:T(8,128)}) fusion(bf16[32,32,8,32]{0,3,2,1:T(8,128)(2,1)} %copy.115, bf16[32,32,8,32]{0,3,2,1:T(8,128)(2,1)} %copy.111), kind=kOutput, calls=%fused_computation.101 | convolution fusion | flops 17563680 | bytes 2129920 | tf_op jit(solution)/shard_map/sub | solution.py:47
  65.3 5.1 %convolution_convert_fusion.1 = bf16[32,8,32,32]{3,2,1,0:T(8,128)(2,1)} fusion(bf16[32,32,8,32]{3,2,1,0:T(8,128)(2,1)S(1)} %copy-done.2, f32[32,8,32,32]{2,3,1,0:T(8,128)} %get-tuple-element.49, f32[32,8,32]{2,1,0:T(8,128)S(1)} %get-tuple-element.48), kind=kOutput, calls=%fused_computation.26 | convolution fusion | flops 17563648 | bytes 2129920 | tf_op jit(solution)/shard_map/phmn,nphe->mphe/dot_general | solution.py:17
  73.3 3.7 %all-to-all-start.3 = ((bf16[32,1,32,256]{3,2,1,0:T(8,128)(2,1)}), bf16[32,1,32,256]{3,2,1,0:T(8,128)(2,1)S(1)}, u32[]{:S(2)}, u32[]{:S(2)}) async-start(bf16[32,1,32,256]{3,2,1,0:T(8,128)(2,1)} %copy.102), calls=%async_computation.3 | async-start | bytes 1048576 | tf_op jit(solution)/shard_map/all_to_all | solution.py:104
  79.0 7.5 %all-to-all-done.3 = bf16[32,1,32,256]{3,2,1,0:T(8,128)(2,1)S(1)} async-done(((bf16[32,1,32,256]{3,2,1,0:T(8,128)(2,1)}), bf16[32,1,32,256]{3,2,1,0:T(8,128)(2,1)S(1)}, u32[]{:S(2)}, u32[]{:S(2)}) %all-to-all-start.3) | async-done | bytes 524320 | tf_op jit(solution)/shard_map/all_to_all | solution.py:104
  93.9 3.5 %all-to-all-start.4 = ((bf16[4,8,32,256]{3,2,0,1:T(8,128)(2,1)}), bf16[4,8,32,256]{3,2,0,1:T(8,128)(2,1)S(1)}, u32[]{:S(2)}, u32[]{:S(2)}) async-start(bf16[4,8,32,256]{3,2,0,1:T(8,128)(2,1)} %copy.108), calls=%async_computation.4 | async-start | bytes 1048576 | tf_op jit(solution)/shard_map/all_to_all | solution.py:123
  97.4 3.3 convolution_bitcast_fusion
  100.7 6.4 %all-to-all-done.4 = bf16[4,8,32,256]{3,2,0,1:T(8,128)(2,1)S(1)} async-done(((bf16[4,8,32,256]{3,2,0,1:T(8,128)(2,1)}), bf16[4,8,32,256]{3,2,0,1:T(8,128)(2,1)S(1)}, u32[]{:S(2)}, u32[]{:S(2)}) %all-to-all-start.4) | async-done | bytes 524320 | tf_op jit(solution)/shard_map/all_to_all | solution.py:123
  109.0 4.2 %copy.121 = bf16[32,32,8,32]{0,3,2,1:T(8,128)(2,1)} copy(bf16[32,32,8,32]{3,2,1,0:T(8,128)(2,1)} %reshape_reshape.31) | data formatting | bytes 1048576 | tf_op jit(solution)/shard_map/reshape;reshape | solution.py:59
  113.2 5.7 %fusion.30 = f32[32,8,32,32]{2,3,1,0:T(8,128)} fusion(bf16[32,32,8,32]{0,3,2,1:T(8,128)(2,1)} %copy.121, bf16[32,32,8,32]{3,2,1,0:T(8,128)(2,1)} %reshape_reshape.27), kind=kOutput, calls=%fused_computation.28 | convolution fusion | flops 16777216 | bytes 2097152 | tf_op jit(solution)/shard_map/mphe,nphe->phmn/dot_general | solution.py:17
  118.8 9.3 %fusion.23 = bf16[32,8,32,32]{3,2,1,0:T(8,128)(2,1)} fusion(bf16[32,32,8,32]{0,3,2,1:T(8,128)(2,1)} %copy.111, f32[32,8,32,32]{2,3,1,0:T(8,128)} %fusion.30, f32[32,8,32,32]{2,3,1,0:T(8,128)} %get-tuple-element.49, f32[32,8,32]{2,1,0:T(8,128)S(1)} %copy-done.24), kind=kOutput, calls=%fused_computation.23 | convolution fusion | flops 18882592 | bytes 3178496 | tf_op jit(solution)/shard_map/phmn,nphe->mphe/dot_general | solution.py:17
  131.0 3.5 %all-to-all-start.5 = ((bf16[32,1,32,256]{3,2,1,0:T(8,128)(2,1)}), bf16[32,1,32,256]{3,2,1,0:T(8,128)(2,1)S(1)}, u32[]{:S(2)}, u32[]{:S(2)}) async-start(bf16[32,1,32,256]{3,2,1,0:T(8,128)(2,1)} %copy.113), calls=%async_computation.5 | async-start | bytes 1048576 | tf_op jit(solution)/shard_map/all_to_all | solution.py:130
  135.6 9.5 %fusion.26 = bf16[32,8,32,32]{3,2,1,0:T(8,128)(2,1)} fusion(bf16[32,32,8,32]{0,3,2,1:T(8,128)(2,1)} %copy.115, f32[32,8,32,32]{2,3,1,0:T(8,128)} %fusion.30, f32[32,8,32,32]{2,3,1,0:T(8,128)} %get-tuple-element.49, f32[32,8,32]{2,1,0:T(8,128)S(1)} %copy-done.24), kind=kOutput, calls=%fused_computation.24 | convolution fusion | flops 18882592 | bytes 3178496 | tf_op jit(solution)/shard_map/phmn,mphe->nphe/dot_general | solution.py:17
  147.9 4.1 %all-to-all-start.6 = ((bf16[32,1,32,256]{3,2,1,0:T(8,128)(2,1)}), bf16[32,1,32,256]{3,2,1,0:T(8,128)(2,1)S(1)}, u32[]{:S(2)}, u32[]{:S(2)}) async-start(bf16[32,1,32,256]{3,2,1,0:T(8,128)(2,1)} %copy.117), calls=%async_computation.6 | async-start | bytes 1048576 | tf_op jit(solution)/shard_map/all_to_all | solution.py:131
  152.1 5.5 %convolution_convert_fusion = bf16[32,8,32,32]{3,2,1,0:T(8,128)(2,1)} fusion(bf16[32,32,8,32]{0,3,2,1:T(8,128)(2,1)} %copy.121, f32[32,8,32,32]{2,3,1,0:T(8,128)} %get-tuple-element.49, f32[32,8,32]{2,1,0:T(8,128)S(1)} %copy-done.24), kind=kOutput, calls=%fused_computation.25 | convolution fusion | flops 17563648 | bytes 2129920 | tf_op jit(solution)/shard_map/phmn,mphe->nphe/dot_general | solution.py:17
  161.8 4.2 %all-to-all-start.7 = ((bf16[32,1,32,256]{3,2,1,0:T(8,128)(2,1)}), bf16[32,1,32,256]{3,2,1,0:T(8,128)(2,1)}, u32[]{:S(2)}, u32[]{:S(2)}) async-start(bf16[32,1,32,256]{3,2,1,0:T(8,128)(2,1)} %copy.123), calls=%async_computation.7 | async-start | bytes 1048576 | tf_op jit(solution)/shard_map/all_to_all | solution.py:132
  166.0 4.7 %fusion.36 = f32[1024,256]{1,0:T(8,128)} fusion(bf16[4,256,256]{2,1,0:T(8,128)(2,1)S(1)} %copy-done.10, f32[4,256,1024]{2,1,0:T(8,128)} %copy-done.5), kind=kOutput, calls=%fused_computation.37 | convolution fusion | flops 546308096 | bytes 5767168 | tf_op jit(solution)/shard_map/mpf,mpd->fd/dot_general | solution.py:17
  170.8 4.9 %all-to-all-done.7 = bf16[32,1,32,256]{3,2,1,0:T(8,128)(2,1)} async-done(((bf16[32,1,32,256]{3,2,1,0:T(8,128)(2,1)}), bf16[32,1,32,256]{3,2,1,0:T(8,128)(2,1)}, u32[]{:S(2)}, u32[]{:S(2)}) %all-to-all-start.7) | async-done | bytes 524320 | tf_op jit(solution)/shard_map/all_to_all | solution.py:132
  182.9 39.6 %all-reduce = (f32[256]{0:T(256)S(1)}, f32[256]{0:T(256)S(1)}) all-reduce(f32[256]{0:T(256)S(1)} %get-tuple-element.38, f32[256]{0:T(256)S(1)} %copy-done.21), channel_id=1, replica_groups=mesh['member'=8,'space'=4] {'member','space'}, use_global_device_ids=true, to_apply=%region_14.0 | all-reduce | flops 512 | bytes 4096 | tf_op jit(solution)/shard_map/psum | solution.py:147
  223.1 96.9 %all-reduce.4.cloned.1.call-done = (f32[256,256]{1,0:T(8,128)}, f32[256,256]{1,0:T(8,128)}, f32[256,256]{1,0:T(8,128)}, f32[256,256]{1,0:T(8,128)}, f32[256,1024]{1,0:T(8,128)}, /*index=5*/f32[1024,256]{1,0:T(8,128)}) async-done(((f32[256,256]{1,0:T(8,128)}, f32[256,256]{1,0:T(8,128)}, f32[256,256]{1,0:T(8,128)}, f32[256,256]{1,0:T(8,128)}, f32[256,1024]{1,0:T(8,128)}, /*index=5*/f32[1024,256]{1,0:T(8,128)}), ...) | async-done | bytes 3145744 | tf_op jit(solution)/shard_map/psum | solution.py:147
  (103 shorter events, 61.3 us)
Async XLA Ops:
  7.2 79.7 %copy-start = (bf16[256,1024]{1,0:T(8,128)(2,1)S(1)}, bf16[256,1024]{1,0:T(8,128)(2,1)}, u32[]{:S(2)}) copy-start(bf16[256,1024]{1,0:T(8,128)(2,1)} %param.18) | copy-start | bytes 1572868
  7.2 8.8 %copy-start.20 = (f32[256]{0:T(256)S(1)}, f32[256]{0:T(256)}, u32[]{:S(2)}) copy-start(f32[256]{0:T(256)} %param.12) | copy-start | bytes 3076
  7.2 8.8 %copy-start.16 = (bf16[256,256]{1,0:T(8,128)(2,1)S(1)}, bf16[256,256]{1,0:T(8,128)(2,1)}, u32[]{:S(2)}) copy-start(bf16[256,256]{1,0:T(8,128)(2,1)} %param.15) | copy-start | bytes 393220
  8.5 20.8 %copy-start.18 = (bf16[256,256]{1,0:T(8,128)(2,1)S(1)}, bf16[256,256]{1,0:T(8,128)(2,1)}, u32[]{:S(2)}) copy-start(bf16[256,256]{1,0:T(8,128)(2,1)} %param.14) | copy-start | bytes 393220
  10.9 14.9 %all-to-all-start.1 = ((bf16[4,8,32,256]{3,2,0,1:T(8,128)(2,1)}), bf16[4,8,32,256]{3,2,0,1:T(8,128)(2,1)S(1)}, u32[]{:S(2)}, u32[]{:S(2)}) async-start(bf16[4,8,32,256]{3,2,0,1:T(8,128)(2,1)} %copy.95), calls=%async_computation.1 | async-start | bytes 1048576 | tf_op jit(solution)/shard_map/all_to_all | solution.py:96
  25.8 19.2 %copy-start.7 = (bf16[4,8,32,256]{3,2,0,1:T(8,128)(2,1)}, bf16[4,8,32,256]{3,2,0,1:T(8,128)(2,1)S(1)}, u32[]{:S(2)}) copy-start(bf16[4,8,32,256]{3,2,0,1:T(8,128)(2,1)S(1)} %all-to-all-done.1) | copy-start | bytes 1572868
  25.8 13.2 %all-to-all-start = ((bf16[4,8,32,256]{3,2,0,1:T(8,128)(2,1)}), bf16[4,8,32,256]{3,2,0,1:T(8,128)(2,1)S(1)}, u32[]{:S(2)}, u32[]{:S(2)}) async-start(bf16[4,8,32,256]{3,2,0,1:T(8,128)(2,1)} %copy.93), calls=%async_computation | async-start | bytes 1048576 | tf_op jit(solution)/shard_map/all_to_all | solution.py:98
  39.0 13.9 %all-to-all-start.2 = ((bf16[4,8,32,256]{3,2,0,1:T(8,128)(2,1)}), bf16[4,8,32,256]{3,2,0,1:T(8,128)(2,1)}, u32[]{:S(2)}, u32[]{:S(2)}) async-start(bf16[4,8,32,256]{3,2,0,1:T(8,128)(2,1)} %copy.97), calls=%async_computation.2 | async-start | bytes 1048576 | tf_op jit(solution)/shard_map/all_to_all | solution.py:97
  58.3 7.0 %copy-start.2 = (bf16[32,32,8,32]{3,2,1,0:T(8,128)(2,1)S(1)}, bf16[32,32,8,32]{3,2,1,0:T(8,128)(2,1)}, u32[]{:S(2)}) copy-start(bf16[32,32,8,32]{3,2,1,0:T(8,128)(2,1)} %reshape_reshape.27) | copy-start | bytes 1572868
  70.4 16.1 %copy-start.11 = (bf16[256,256]{1,0:T(8,128)(2,1)S(1)}, bf16[256,256]{1,0:T(8,128)(2,1)}, u32[]{:S(2)}) copy-start(bf16[256,256]{1,0:T(8,128)(2,1)} %param.16) | copy-start | bytes 393220
  70.4 16.5 %copy-start.19 = (f32[256]{0:T(256)S(1)}, f32[256]{0:T(256)}, u32[]{:S(2)}) copy-start(f32[256]{0:T(256)} %param.17) | copy-start | bytes 3076
  73.3 13.2 %all-to-all-start.3 = ((bf16[32,1,32,256]{3,2,1,0:T(8,128)(2,1)}), bf16[32,1,32,256]{3,2,1,0:T(8,128)(2,1)S(1)}, u32[]{:S(2)}, u32[]{:S(2)}) async-start(bf16[32,1,32,256]{3,2,1,0:T(8,128)(2,1)} %copy.102), calls=%async_computation.3 | async-start | bytes 1048576 | tf_op jit(solution)/shard_map/all_to_all | solution.py:104
  93.9 13.2 %all-to-all-start.4 = ((bf16[4,8,32,256]{3,2,0,1:T(8,128)(2,1)}), bf16[4,8,32,256]{3,2,0,1:T(8,128)(2,1)S(1)}, u32[]{:S(2)}, u32[]{:S(2)}) async-start(bf16[4,8,32,256]{3,2,0,1:T(8,128)(2,1)} %copy.108), calls=%async_computation.4 | async-start | bytes 1048576 | tf_op jit(solution)/shard_map/all_to_all | solution.py:123
  113.2 5.7 %copy-start.24 = (f32[32,8,32]{2,1,0:T(8,128)S(1)}, f32[32,8,32]{2,1,0:T(8,128)}, u32[]{:S(2)}) copy-start(f32[32,8,32]{2,1,0:T(8,128)} %copy-done.23) | copy-start | bytes 98308
  118.8 15.7 %copy-start.4 = (bf16[4,8,1,32,256]{4,3,1,0,2:T(8,128)(2,1)S(1)}, bf16[4,8,1,32,256]{4,3,1,0,2:T(8,128)(2,1)}, u32[]{:S(2)}) copy-start(bf16[4,8,1,32,256]{4,3,1,0,2:T(8,128)(2,1)} %copy-done.3) | copy-start | bytes 1572868
  131.0 16.9 %all-to-all-start.5 = ((bf16[32,1,32,256]{3,2,1,0:T(8,128)(2,1)}), bf16[32,1,32,256]{3,2,1,0:T(8,128)(2,1)S(1)}, u32[]{:S(2)}, u32[]{:S(2)}) async-start(bf16[32,1,32,256]{3,2,1,0:T(8,128)(2,1)} %copy.113), calls=%async_computation.5 | async-start | bytes 1048576 | tf_op jit(solution)/shard_map/all_to_all | solution.py:130
  147.9 13.9 %all-to-all-start.6 = ((bf16[32,1,32,256]{3,2,1,0:T(8,128)(2,1)}), bf16[32,1,32,256]{3,2,1,0:T(8,128)(2,1)S(1)}, u32[]{:S(2)}, u32[]{:S(2)}) async-start(bf16[32,1,32,256]{3,2,1,0:T(8,128)(2,1)} %copy.117), calls=%async_computation.6 | async-start | bytes 1048576 | tf_op jit(solution)/shard_map/all_to_all | solution.py:131
  152.1 14.0 %copy-start.10 = (bf16[4,256,256]{2,1,0:T(8,128)(2,1)S(1)}, bf16[4,256,256]{2,1,0:T(8,128)(2,1)}, u32[]{:S(2)}) copy-start(bf16[4,256,256]{2,1,0:T(8,128)(2,1)} %param.11) | copy-start | bytes 1572868
  161.8 13.9 %all-to-all-start.7 = ((bf16[32,1,32,256]{3,2,1,0:T(8,128)(2,1)}), bf16[32,1,32,256]{3,2,1,0:T(8,128)(2,1)}, u32[]{:S(2)}, u32[]{:S(2)}) async-start(bf16[32,1,32,256]{3,2,1,0:T(8,128)(2,1)} %copy.123), calls=%async_computation.7 | async-start | bytes 1048576 | tf_op jit(solution)/shard_map/all_to_all | solution.py:132
  166.0 154.0 %all-reduce.4.cloned.1.call-start = ((), (), s32[]{:S(2)}) async-start(), calls=%async_computation.8 | async-start | bytes 6291456 | tf_op jit(solution)/shard_map/psum | solution.py:147
  181.3 145.1 %copy-start.1 = (bf16[256,1024]{1,0:T(8,128)(2,1)S(1)}, bf16[256,1024]{1,0:T(8,128)(2,1)}, u32[]{:S(2)}) copy-start(bf16[256,1024]{1,0:T(8,128)(2,1)} %param.18) | copy-start | bytes 1572868
  320.0 4.7 %copy-start.15 = (f32[256,256]{1,0:T(8,128)S(1)}, f32[256,256]{1,0:T(8,128)}, u32[]{:S(2)}) copy-start(f32[256,256]{1,0:T(8,128)} %get-tuple-element.43) | copy-start | bytes 786436
  320.0 5.6 %copy-start.12 = (f32[256,256]{1,0:T(8,128)S(1)}, f32[256,256]{1,0:T(8,128)}, u32[]{:S(2)}) copy-start(f32[256,256]{1,0:T(8,128)} %get-tuple-element.44) | copy-start | bytes 786436
  320.0 5.6 %copy-start.13 = (f32[256,256]{1,0:T(8,128)S(1)}, f32[256,256]{1,0:T(8,128)}, u32[]{:S(2)}) copy-start(f32[256,256]{1,0:T(8,128)} %get-tuple-element.45) | copy-start | bytes 786436
  (10 other events, 24.1 us)
Sparse Core Ops, SparseCore 0:
  180.1 139.8 all-reduce.3
where the time goes:
time: 335 us; the launch traced here: 333 us
  waiting for transfers between devices  136 us (41%)
  matrix products  63 us (19%)
  local copies, waits for them, and re-layouts  40.3 us (12%)
  blocking collectives  39.6 us (12%)
  starting transfers between devices  31.8 us (9%)
  between operations  14.4 us (4%)
  other arithmetic  7.74 us (2%)
    psum x1, waiting for transfers between devices, on_device(): lax.psum((part_query, part_key, part_value, part_wout, part_up, part_down...  96.9 us
    dot_general x22, matrix products, multiply(): return jnp.einsum(form, left, right, preferred_element_type=jnp.float32)  56.7 us
    psum x1, blocking collectives, on_device(): lax.psum((part_query, part_key, part_value, part_wout, part_up, part_down...  39.6 us
    another operation x4, local copies, waits for them, and re-layouts, memberwise(): return array.reshape(everyone, 1, spread, array.shape[-1])  11.4 us
    all_to_all x1, waiting for transfers between devices, on_device(): lax.all_to_all(patchwise(query), 'member', split_axis=1, concat_axis=0, t...  8.46 us
    all_to_all x1, waiting for transfers between devices, on_device(): lax.all_to_all(patchwise(values), 'member', split_axis=1, concat_axis=0,...  8.39 us
    all_to_all x1, waiting for transfers between devices, on_device(): lax.all_to_all(memberwise(mixed_here), 'member', split_axis=0, concat_axi...  7.45 us
  transfers between devices with their start and end apart: 9, of which 8 were waited for; matrix products, arithmetic and copies ran while one was open for 14% of the time, Pallas kernels for 0%

commit v1 on v0

v1 whole, which is shorter than its diff:
```python
import functools
import math

import jax
import jax.numpy as jnp
from jax import lax
from jax.experimental import pallas as pl
from jax.experimental.pallas import tpu as pltpu
from jax.sharding import PartitionSpec as P

HEAD_DIM = 32
EPS = 1e-06
GELU_C = 0.7978845608028654
GELU_A = 0.044715
F32 = jnp.float32
BF16 = jnp.bfloat16


def dot(left, right):
    return lax.dot_general(left, right, (((1,), (0,)), ((), ())), preferred_element_type=F32)


def dot_nt(left, right):
    return lax.dot_general(left, right, (((1,), (1,)), ((), ())), preferred_element_type=F32)


def dot_tn(left, right):
    return lax.dot_general(left, right, (((0,), (0,)), ((), ())), preferred_element_type=F32)


def norm_rows(values):
    inverse = lax.rsqrt(jnp.mean(values * values, axis=-1, keepdims=True) + EPS)
    return values * inverse, inverse


def norm_back(unit_rows, inverse, gains, upstream):
    scaled = upstream * gains
    return inverse * (scaled - unit_rows * jnp.mean(scaled * unit_rows, axis=-1, keepdims=True))


def gelu_pair(preact):
    square = preact * preact
    tangent = jnp.tanh(GELU_C * (preact + GELU_A * preact * square))
    half = 0.5 * (1.0 + tangent)
    slopes = half + 0.5 * preact * (1.0 - tangent * tangent) * (
        GELU_C + (3.0 * GELU_A * GELU_C) * square
    )
    return preact * half, slopes


class Layer:
    def __init__(self, members, patches, width, hidden):
        self.members, self.patches, self.width, self.hidden = members, patches, width, hidden
        self.heads = width // HEAD_DIM
        self.groups, self.rows = patches // 8, members * 8
        self.tokens = self.groups * self.rows
        self.scale = 1.0 / math.sqrt(HEAD_DIM)

    def scratch(self):
        groups, rows, width, hidden = self.groups, self.rows, self.width, self.hidden
        return dict(
            x=pltpu.VMEM((groups, rows, width), F32),
            og=pltpu.VMEM((groups, rows, width), BF16),
            n1=pltpu.VMEM((groups, rows, width), BF16),
            q=pltpu.VMEM((groups, rows, width), BF16),
            k=pltpu.VMEM((groups, rows, width), BF16),
            v=pltpu.VMEM((groups, rows, width), BF16),
            mix=pltpu.VMEM((groups, rows, width), BF16),
            n2=pltpu.VMEM((groups, rows, width), BF16),
            act=pltpu.VMEM((groups, rows, hidden), BF16),
            pre=pltpu.VMEM((groups, rows, hidden), BF16),
            ga=pltpu.VMEM((groups, rows, width), BF16),
            gm=pltpu.VMEM((groups, rows, width), BF16),
            gh=pltpu.VMEM((groups, rows, width), F32),
            gq=pltpu.VMEM((groups, rows, width), BF16),
            gk=pltpu.VMEM((groups, rows, width), BF16),
            gv=pltpu.VMEM((groups, rows, width), BF16),
            p=pltpu.VMEM((groups, self.heads, rows, rows), F32),
        )

    def head_mask(self, head):
        lanes = lax.broadcasted_iota(jnp.int32, (1, self.width), 1)
        inside = (lanes >= head * HEAD_DIM) & (lanes < (head + 1) * HEAD_DIM)
        return jnp.where(inside, 1.0, 0.0).astype(BF16)

    def regroup(self, source, target):
        for pair in range(self.groups // 2):
            block = source[:, 16 * pair : 16 * pair + 16, :].astype(F32)
            for half in range(2):
                piece = block[:, 8 * half : 8 * half + 8, :].reshape(self.rows, self.width)
                target[2 * pair + half] = piece.astype(target.dtype)

    def ungroup(self, source, target):
        for pair in range(self.groups // 2):
            halves = [
                source[2 * pair + half].reshape(self.members, 8, self.width) for half in range(2)
            ]
            target[:, 16 * pair : 16 * pair + 16, :] = jnp.concatenate(halves, axis=1).astype(
                target.dtype
            )

    def attention(self, s, w, g):
        unit, _ = norm_rows(s["x"][g])
        normed = (unit * w["g1"][...]).astype(BF16)
        s["n1"][g] = normed
        query = dot(normed, w["wq"][...]).astype(BF16)
        keys = dot(normed, w["wk"][...]).astype(BF16)
        values = dot(normed, w["wv"][...]).astype(BF16)
        s["q"][g], s["k"][g], s["v"][g] = query, keys, values
        rows = self.rows
        same = (
            lax.broadcasted_iota(jnp.int32, (rows, rows), 0) % 8
            == lax.broadcasted_iota(jnp.int32, (rows, rows), 1) % 8
        )
        mixed = jnp.zeros((rows, self.width), F32)
        for head in range(self.heads):
            mask = self.head_mask(head)
            scores = jnp.where(same, dot_nt(query * mask, keys) * self.scale, -1e30)
            weights = jnp.exp(scores - jnp.max(scores, axis=-1, keepdims=True))
            weights = weights * (1.0 / jnp.sum(weights, axis=-1, keepdims=True))
            s["p"][g, head] = weights
            mixed += dot(weights.astype(BF16), values * mask)
        s["mix"][g] = mixed.astype(BF16)

    def feed_forward(self, s, w, g, gain2):
        mixed, out_grad = s["mix"][g], s["og"][g]
        state = s["x"][g] + dot(mixed, w["wo"][...])
        unit, inverse = norm_rows(state)
        normed = (unit * w["g2"][...]).astype(BF16)
        s["n2"][g] = normed
        grad_normed = jnp.zeros((self.rows, self.width), F32)
        step = 256
        for at in range(0, self.hidden, step):
            some = slice(at, at + step)
            activated, slopes = gelu_pair(dot(normed, w["wu"][:, some]))
            s["act"][g, :, some] = activated.astype(BF16)
            grad_pre = (dot_nt(out_grad, w["wd"][some, :]) * slopes).astype(BF16)
            s["pre"][g, :, some] = grad_pre
            grad_normed += dot_nt(grad_pre, w["wu"][:, some])
        grad_hidden = out_grad.astype(F32) + norm_back(unit, inverse, w["g2"][...], grad_normed)
        s["gh"][g] = grad_hidden
        grad_attn = grad_hidden.astype(BF16)
        s["ga"][g] = grad_attn
        s["gm"][g] = dot_nt(grad_attn, w["wo"][...]).astype(BF16)
        return gain2 + jnp.sum(grad_normed * unit, axis=0, keepdims=True)

    def attention_back(self, s, w, g, gain1):
        query, keys, values, upstream = s["q"][g], s["k"][g], s["v"][g], s["gm"][g]
        grad_q = jnp.zeros((self.rows, self.width), F32)
        grad_k, grad_v = grad_q, grad_q
        for head in range(self.heads):
            mask = self.head_mask(head)
            weights = s["p"][g, head]
            up = upstream * mask
            dprob = dot_nt(up, values)
            both = weights * dprob
            dscore = both - weights * jnp.sum(both, axis=-1, keepdims=True)
            dscore = (dscore * self.scale).astype(BF16)
            grad_v += dot_tn(weights.astype(BF16), up)
            grad_q += dot(dscore, keys * mask)
            grad_k += dot_tn(dscore, query * mask)
        grad_q, grad_k, grad_v = (grad.astype(BF16) for grad in (grad_q, grad_k, grad_v))
        s["gq"][g], s["gk"][g], s["gv"][g] = grad_q, grad_k, grad_v
        grad_normed = (
            dot_nt(grad_q, w["wq"][...])
            + dot_nt(grad_k, w["wk"][...])
            + dot_nt(grad_v, w["wv"][...])
        )
        unit, inverse = norm_rows(s["x"][g])
        back = norm_back(unit, inverse, w["g1"][...], grad_normed)
        s["gh"][g] = (s["gh"][g] - s["og"][g].astype(F32)) + back
        return gain1 + jnp.sum(grad_normed * unit, axis=0, keepdims=True)

    def flat(self, s, name):
        array = s[name][...]
        return array.reshape(self.tokens, array.shape[-1])

    def wide_parts(self, s, parts):
        out_grad, normed = self.flat(s, "og"), self.flat(s, "n2")
        for at in range(0, self.hidden, 256):
            some = slice(at, at + 256)
            act = s["act"][:, :, some].reshape(self.tokens, 256)
            parts[some, :] = dot_tn(act, out_grad)
            pre = s["pre"][:, :, some].reshape(self.tokens, 256)
            parts[self.hidden + at : self.hidden + at + 256, :] = dot_tn(normed, pre)

    def square_parts(self, s, parts):
        normed = self.flat(s, "n1")
        at = 2 * self.hidden
        for name in ("gq", "gk", "gv"):
            parts[at : at + self.width, :] = dot_tn(normed, self.flat(s, name))
            at += self.width
        parts[at : at + self.width, :] = dot_tn(self.flat(s, "mix"), self.flat(s, "ga"))


WEIGHTS = ("g1", "wq", "wk", "wv", "wo", "g2", "wu", "wd")


def kernel(layer, names, *refs):
    x_ref, og_ref = refs[:2]
    w = dict(zip(WEIGHTS, refs[2:10]))
    y_ref, parts_ref, gains_ref = refs[10:13]
    s = dict(zip(names, refs[13:]))
    layer.regroup(x_ref, s["x"])
    layer.regroup(og_ref, s["og"])
    zero = jnp.zeros((1, layer.width), F32)

    @pl.loop(0, layer.groups)
    def _(g):
        layer.attention(s, w, g)

    gain2 = lax.fori_loop(0, layer.groups, lambda g, c: layer.feed_forward(s, w, g, c), zero)
    layer.wide_parts(s, parts_ref)
    gain1 = lax.fori_loop(0, layer.groups, lambda g, c: layer.attention_back(s, w, g, c), zero)
    layer.square_parts(s, parts_ref)
    layer.ungroup(s["gh"], y_ref)
    gains_ref[0:1, :] = gain1
    gains_ref[1:2, :] = gain2


def on_device(x, og, g1, wq, wk, wv, wo, g2, wu, wd):
    groups = lax.axis_size("member")
    own_members, own_patches, width = x.shape
    spread = own_patches // groups
    everyone = own_members * groups
    hidden = wu.shape[1]
    layer = Layer(everyone, spread, width, hidden)

    def patchwise(array):
        array = array.reshape(own_members, groups, spread, width)
        array = lax.all_to_all(array, "member", split_axis=1, concat_axis=0, tiled=True)
        return array.reshape(everyone, spread, width)

    scratch = layer.scratch()
    vmem = pl.BlockSpec(memory_space=pltpu.VMEM)
    back, parts, gains = pl.pallas_call(
        functools.partial(kernel, layer, tuple(scratch)),
        out_shape=(
            jax.ShapeDtypeStruct((everyone, spread, width), BF16),
            jax.ShapeDtypeStruct((2 * hidden + 4 * width, width), F32),
            jax.ShapeDtypeStruct((2, width), F32),
        ),
        in_specs=[vmem] * 10,
        out_specs=(vmem, vmem, vmem),
        scratch_shapes=list(scratch.values()),
        compiler_params=pltpu.CompilerParams(vmem_limit_bytes=60 * 2**20),
    )(patchwise(x), patchwise(og), g1.reshape(1, width), wq, wk, wv, wo, g2.reshape(1, width), wu, wd)
    back = lax.all_to_all(
        back.reshape(everyone, 1, spread, width), "member", split_axis=0, concat_axis=1, tiled=True
    ).reshape(own_members, own_patches, width)
    input_grad = og.astype(F32) + back.astype(F32)
    scale = 1.0 / math.sqrt(everyone * own_patches * lax.axis_size("space"))
    parts, gains = lax.psum((parts, gains), ("member", "space"))
    return finish(input_grad, parts * scale, gains * scale, width, hidden)


def finish(input_grad, parts, gains, width, hidden):
    down = parts[:hidden]
    up = parts[hidden : 2 * hidden].reshape(hidden // width, width, width)
    up = up.transpose(1, 0, 2).reshape(width, hidden)
    squares = [parts[2 * hidden + width * i : 2 * hidden + width * (i + 1)] for i in range(4)]
    return (input_grad, *squares, up, down, gains[0], gains[1])


def solution(mesh):
    spread = P("member", "space", None)
    return jax.shard_map(
        on_device,
        mesh=mesh,
        in_specs=(spread, spread) + (P(),) * 8,
        out_specs=(spread,) + (P(),) * 8,
        check_vma=False,
    )
```

time: 335 us -> 218 us (0.65)
  matrix products: 63 us -> 0 us
  waiting for transfers between devices: 136 us -> 95.7 us
  local copies, waits for them, and re-layouts: 40.3 us -> 6.8 us
  Pallas kernels: 0 us -> 29 us
  starting transfers between devices: 31.8 us -> 8.84 us
  blocking collectives: 39.6 us -> 60.1 us
  other arithmetic: 7.74 us -> 3.37 us
    dot_general x22 -> x0, matrix products: 56.7 us -> none  [multiply(): return jnp.einsum(form, left, right, preferred_element_type=jnp.float32)]
    all_to_all x8 -> x2, waiting for transfers between devices: 39.4 us -> 8.62 us  [the longest x1 8.62 us: patchwise(): lax.all_to_all(array, 'member', split_axis=1, concat_axis=0, tiled=True)]
    another operation x11 -> x0, local copies, waits for them, and re-layouts: 30.3 us -> none  [the longest x4 11.4 us: memberwise(): return array.reshape(everyone, 1, spread, array.shape[-1])]
    pallas_call x0 -> x1, Pallas kernels: none -> 29 us  [on_device(): pl.pallas_call(functools.partial(kernel, layer, tuple(scratch)), out_shap...]
    all_to_all x8 -> x2, starting transfers between devices: 31.8 us -> 8.81 us  [the longest x1 5.17 us: patchwise(): lax.all_to_all(array, 'member', split_axis=1, concat_axis=0, tiled=True)]
    all_to_all x0 -> x1, blocking collectives: none -> 12.8 us  [patchwise(): lax.all_to_all(array, 'member', split_axis=1, concat_axis=0, tiled=True)]
    psum x1, waiting for transfers between devices: 96.9 us -> 87.1 us  [on_device(): parts, gains = lax.psum((parts, gains), ('member', 'space'))]
    psum x1, blocking collectives: 39.6 us -> 47.2 us  [on_device(): parts, gains = lax.psum((parts, gains), ('member', 'space'))]
  transfers between devices with their start and end apart: 9 -> 3, of which waited for: 8 -> 2; matrix products, arithmetic and copies ran while one was open for 14% -> 1% of each run, Pallas kernels for 0% -> 0%
where the time goes in v1:
time: 218 us
  waiting for transfers between devices  95.7 us (44%)
  blocking collectives  60.1 us (28%)
  Pallas kernels  29 us (13%)
  between operations  14.1 us (6%)
  starting transfers between devices  8.84 us (4%)
  local copies, waits for them, and re-layouts  6.8 us (3%)
  other arithmetic  3.37 us (2%)
    psum x1, waiting for transfers between devices, on_device(): parts, gains = lax.psum((parts, gains), ('member', 'space'))  87.1 us
    psum x1, blocking collectives, on_device(): parts, gains = lax.psum((parts, gains), ('member', 'space'))  47.2 us
    pallas_call x1, Pallas kernels, on_device(): pl.pallas_call(functools.partial(kernel, layer, tuple(scratch)), out_shap...  29 us
    all_to_all x1, blocking collectives, patchwise(): lax.all_to_all(array, 'member', split_axis=1, concat_axis=0, tiled=True)  12.8 us
    all_to_all x1, waiting for transfers between devices, patchwise(): lax.all_to_all(array, 'member', split_axis=1, concat_axis=0, tiled=True)  8.62 us
    all_to_all x1, starting transfers between devices, patchwise(): lax.all_to_all(array, 'member', split_axis=1, concat_axis=0, tiled=True)  5.17 us
  transfers between devices with their start and end apart: 3, of which 2 were waited for; matrix products, arithmetic and copies ran while one was open for 1% of the time, Pallas kernels for 0%

profile of v1, /device:TPU:0, one launch (start us, length us, event | category | flops | bytes accessed | tf_op | source)
XLA Modules:
  0.0 217.9 jit_solution(12141803335908589733)
XLA Ops:
  7.2 1.9 copy.23
  9.1 5.2 %all-to-all-start = ((bf16[4,8,32,256]{3,2,0,1:T(8,128)(2,1)}), bf16[4,8,32,256]{3,2,0,1:T(8,128)(2,1)S(1)}, u32[]{:S(2)}, u32[]{:S(2)}) async-start(bf16[4,8,32,256]{3,2,0,1:T(8,128)(2,1)} %copy.23), calls=%async_computation | async-start | bytes 1048576 | tf_op jit(solution)/shard_map/all_to_all | solution.py:231
  14.2 0.0 all-reduce.2.cloned.1.call-start
  14.3 1.1 copy.24
  15.4 8.6 %all-to-all-done = bf16[4,8,32,256]{3,2,0,1:T(8,128)(2,1)S(1)} async-done(((bf16[4,8,32,256]{3,2,0,1:T(8,128)(2,1)}), bf16[4,8,32,256]{3,2,0,1:T(8,128)(2,1)S(1)}, u32[]{:S(2)}, u32[]{:S(2)}) %all-to-all-start) | async-done | bytes 524320 | tf_op jit(solution)/shard_map/all_to_all | solution.py:231
  24.0 12.8 %all_to_all.39 = bf16[4,8,32,256]{3,2,0,1:T(8,128)(2,1)} all-to-all(bf16[4,8,32,256]{3,2,0,1:T(8,128)(2,1)S(1)} %copy.24), channel_id=1, replica_groups=mesh['member'=8,'space'=4] {'member'}, dimensions={1} | all-to-all | bytes 1048576 | tf_op jit(solution)/shard_map/all_to_all | solution.py:231
  36.8 0.0 copy-done.1
  36.8 29.0 %shard_map.169 = (bf16[32,32,256]{2,1,0:T(8,128)(2,1)}, f32[3072,256]{1,0:T(8,128)}, f32[2,256]{1,0:T(2,128)}) custom-call(bf16[32,32,256]{2,1,0:T(8,128)(2,1)} %bitcast.33, bf16[32,32,256]{2,1,0:T(8,128)(2,1)} %bitcast.34, f32[1,256]{1,0:T(1,128)} %bitcast.37, bf16[256,256]{1,0:T(8,128)(2,1)} %refs_3_.1, bf16[256,256]{1,0:T(8,128)(2,1)} %refs_4_.1, ...), custom_call_target="tpu_custom_call" | custom-call | tf_op jit(solution)/shard_map/pallas_call | solution.py:236
  65.8 0.0 all-reduce.2.cloned.1.call-update
  65.8 0.0 copy-start
  65.9 3.6 %all-to-all-start.2 = ((bf16[32,1,32,256]{3,2,1,0:T(8,128)(2,1)}), bf16[32,1,32,256]{3,2,1,0:T(8,128)(2,1)S(1)}, u32[]{:S(2)}, u32[]{:S(2)}) async-start(bf16[32,1,32,256]{3,2,1,0:T(8,128)(2,1)} %bitcast.11), calls=%async_computation.2 | async-start | bytes 1048576 | tf_op jit(solution)/shard_map/all_to_all | solution.py:248
  69.5 0.0 copy-done.2
  69.5 47.2 %psum.15 = f32[2,256]{1,0:T(2,128)S(1)} all-reduce(f32[2,256]{1,0:T(2,128)S(1)} %copy-done.2), channel_id=1, replica_groups=mesh['member'=8,'space'=4] {'member','space'}, use_global_device_ids=true, to_apply=%region_1.0 | all-reduce | flops 512 | bytes 4096 | tf_op jit(solution)/shard_map/psum | solution.py:253
  116.7 0.6 fusion.2
  117.3 0.0 all-to-all-done.2
  117.3 0.1 convert_bitcast_fusion
  117.4 0.1 copy.26
  117.5 0.0 copy-done
  117.5 1.1 convert_add_fusion
  118.6 87.1 %all-reduce.2.cloned.1.call-done = f32[3072,256]{1,0:T(8,128)} async-done(((f32[3072,256]{1,0:T(8,128)}), f32[3072,256]{1,0:T(8,128)}) %all-reduce.2.cloned.1.call-update) | async-done | bytes 3145744 | tf_op jit(solution)/shard_map/psum | solution.py:253
  205.7 2.2 broadcast_multiply_fusion
  207.9 1.0 fusion.1
  208.8 1.1 fusion
  209.9 1.1 copy.28
  (3 shorter events, 0.0 us)
Async XLA Ops:
  9.1 14.9 %all-to-all-start = ((bf16[4,8,32,256]{3,2,0,1:T(8,128)(2,1)}), bf16[4,8,32,256]{3,2,0,1:T(8,128)(2,1)S(1)}, u32[]{:S(2)}, u32[]{:S(2)}) async-start(bf16[4,8,32,256]{3,2,0,1:T(8,128)(2,1)} %copy.23), calls=%async_computation | async-start | bytes 1048576 | tf_op jit(solution)/shard_map/all_to_all | solution.py:231
  14.2 191.5 %all-reduce.2.cloned.1.call-start = ((), (), s32[]{:S(2)}) async-start(), calls=%async_computation.3 | async-start | bytes 6291456 | tf_op jit(solution)/shard_map/psum | solution.py:253
  24.0 12.8 %copy-start.1 = (bf16[4,8,32,256]{3,2,0,1:T(8,128)(2,1)}, bf16[4,8,32,256]{3,2,0,1:T(8,128)(2,1)S(1)}, u32[]{:S(2)}) copy-start(bf16[4,8,32,256]{3,2,0,1:T(8,128)(2,1)S(1)} %all-to-all-done) | copy-start | bytes 1572868
  65.8 3.7 %copy-start.2 = (f32[2,256]{1,0:T(2,128)S(1)}, f32[2,256]{1,0:T(2,128)}, u32[]{:S(2)}) copy-start(f32[2,256]{1,0:T(2,128)} %get-tuple-element.14) | copy-start | bytes 6148
  65.8 51.7 %copy-start = (bf16[4,256,256]{2,1,0:T(8,128)(2,1)S(1)}, bf16[4,256,256]{2,1,0:T(8,128)(2,1)}, u32[]{:S(2)}) copy-start(bf16[4,256,256]{2,1,0:T(8,128)(2,1)} %param.11) | copy-start | bytes 1572868
  65.9 51.5 %all-to-all-start.2 = ((bf16[32,1,32,256]{3,2,1,0:T(8,128)(2,1)}), bf16[32,1,32,256]{3,2,1,0:T(8,128)(2,1)S(1)}, u32[]{:S(2)}, u32[]{:S(2)}) async-start(bf16[32,1,32,256]{3,2,1,0:T(8,128)(2,1)} %bitcast.11), calls=%async_computation.2 | async-start | bytes 1048576 | tf_op jit(solution)/shard_map/all_to_all | solution.py:248
Sparse Core Ops, SparseCore 0:
  66.0 139.6 all-reduce.1

commit v2 on v1

--- a/solution.py
+++ b/solution.py
@@ -183,14 +183,21 @@
             parts[some, :] = dot_tn(act, out_grad)
             pre = s["pre"][:, :, some].reshape(self.tokens, 256)
             parts[self.hidden + at : self.hidden + at + 256, :] = dot_tn(normed, pre)
+        self.clear_rest(parts, 2 * self.hidden)
 
     def square_parts(self, s, parts):
         normed = self.flat(s, "n1")
-        at = 2 * self.hidden
+        at = 0
         for name in ("gq", "gk", "gv"):
             parts[at : at + self.width, :] = dot_tn(normed, self.flat(s, name))
             at += self.width
         parts[at : at + self.width, :] = dot_tn(self.flat(s, "mix"), self.flat(s, "ga"))
+        self.clear_rest(parts, at + self.width)
+
+    def clear_rest(self, parts, used):
+        rest = parts.shape[0] - used
+        if rest:
+            parts[used:, :] = jnp.zeros((rest, self.width), F32)
 
 
 WEIGHTS = ("g1", "wq", "wk", "wv", "wo", "g2", "wu", "wd")
@@ -199,8 +206,8 @@
 def kernel(layer, names, *refs):
     x_ref, og_ref = refs[:2]
     w = dict(zip(WEIGHTS, refs[2:10]))
-    y_ref, parts_ref, gains_ref = refs[10:13]
-    s = dict(zip(names, refs[13:]))
+    y_ref, wide_ref, square_ref, gains_ref = refs[10:14]
+    s = dict(zip(names, refs[14:]))
     layer.regroup(x_ref, s["x"])
     layer.regroup(og_ref, s["og"])
     zero = jnp.zeros((1, layer.width), F32)
@@ -210,56 +217,375 @@
         layer.attention(s, w, g)
 
     gain2 = lax.fori_loop(0, layer.groups, lambda g, c: layer.feed_forward(s, w, g, c), zero)
-    layer.wide_parts(s, parts_ref)
+    layer.wide_parts(s, wide_ref)
     gain1 = lax.fori_loop(0, layer.groups, lambda g, c: layer.attention_back(s, w, g, c), zero)
-    layer.square_parts(s, parts_ref)
+    layer.square_parts(s, square_ref)
     layer.ungroup(s["gh"], y_ref)
+    gains_ref[...] = jnp.zeros_like(gains_ref)
     gains_ref[0:1, :] = gain1
     gains_ref[1:2, :] = gain2
 
 
+class Ring:
+    def __init__(self):
+        self.member, self.space = lax.axis_index("member"), lax.axis_index("space")
+        self.members, self.spaces = lax.axis_size("member"), lax.axis_size("space")
+        self.chips = self.members // 2
+        self.core = lax.rem(self.member, 2)
+        self.chip = self.member // 2
+
+    def member_peer(self, off):
+        return lax.rem(self.member + off, self.members)
+
+    def sibling(self):
+        return self.member + 1 - 2 * self.core
+
+    def chip_peer(self, off):
+        return lax.rem(self.chip + off, self.chips)
+
+    def space_peer(self, off):
+        return lax.rem(self.space + off, self.spaces)
+
+    def barrier(self, along_space):
+        barrier = pltpu.get_barrier_semaphore()
+        targets = [(self.member_peer(off), self.space) for off in range(1, self.members)]
+        if along_space:
+            targets += [(self.member, self.space_peer(off)) for off in range(1, self.spaces)]
+        for target in targets:
+            pl.semaphore_signal(
+                barrier, inc=1, device_id=target, device_id_type=pl.DeviceIdType.MESH
+            )
+        pl.semaphore_wait(barrier, len(targets))
+
+
+def send(source, target, sems, slot, device):
+    copy = pltpu.make_async_remote_copy(
+        src_ref=source,
+        dst_ref=target,
+        send_sem=sems.at[0, slot],
+        recv_sem=sems.at[1, slot],
+        device_id=device,
+        device_id_type=pl.DeviceIdType.MESH,
+    )
+    copy.start()
+    return copy
+
+
+def some_rows(start, size):
+    return pl.ds(pl.multiple_of(start, 16), size)
+
+
+class Exchange:
+    def __init__(self, ring, own, spread):
+        self.ring, self.own, self.spread = ring, own, spread
+
+    def mine(self, ref, index):
+        return ref.at[:, some_rows(index * self.spread, self.spread), :]
+
+    def here(self, ref, index):
+        return ref.at[pl.ds(index * self.own, self.own), :, :]
+
+    def start(self, source, target, sems, local, to_patch):
+        ring = self.ring
+        take, put = (self.mine, self.here) if to_patch else (self.here, self.mine)
+        self.copies = []
+        for off in range(1, ring.members):
+            peer = ring.member_peer(off)
+            self.copies.append(
+                send(take(source, peer), put(target, ring.member), sems, off, (peer, ring.space))
+            )
+        own = pltpu.make_async_copy(take(source, ring.member), put(target, ring.member), local)
+        own.start()
+        self.copies.append(own)
+        return self
+
+    def wait(self):
+        for copy in self.copies:
+            copy.wait()
+
+
+class Total:
+    def __init__(self, ring, scale, parts, full, recv_a, send_b, recv_b, send_c, recv_c, own, sems):
+        self.ring, self.scale = ring, scale
+        self.parts, self.full, self.sems, self.own = parts, full, sems, own
+        self.recv_a, self.send_b, self.recv_b = recv_a, send_b, recv_b
+        self.send_c, self.recv_c = send_c, recv_c
+        self.rows_a = parts.shape[0] // 2
+        self.rows_b = self.rows_a // ring.chips
+        self.rows_c = self.rows_b // ring.spaces
+        self.at_a = ring.core * self.rows_a
+        self.at_b = self.at_a + ring.chip * self.rows_b
+        self.at_c = self.at_b + ring.space * self.rows_c
+
+    @staticmethod
+    def scratch(rows, width, chips, spaces):
+        a = rows // 2
+        b = a // chips
+        c = b // spaces
+        slots = 2 * (chips + spaces)
+        return [
+            pltpu.VMEM((rows, width), BF16),
+            pltpu.VMEM((a, width), F32),
+            pltpu.VMEM((a, width), BF16),
+            pltpu.VMEM((chips, b, width), BF16),
+            pltpu.VMEM((b, width), BF16),
+            pltpu.VMEM((spaces, c, width), BF16),
+            pltpu.VMEM((b, width), F32),
+            pltpu.SemaphoreType.DMA((2, slots)),
+        ]
+
+    def start(self):
+        ring = self.ring
+        other = some_rows((1 - ring.core) * self.rows_a, self.rows_a)
+        self.copies = [
+            send(self.parts.at[other], self.recv_a, self.sems, 0, (ring.sibling(), ring.space))
+        ]
+
+    def wait(self):
+        for copy in self.copies:
+            copy.wait()
+
+    def to_chips(self):
+        ring = self.ring
+        self.wait()
+        self.copies = []
+        for off in range(1, ring.chips):
+            peer = ring.chip_peer(off)
+            at = peer * self.rows_b
+            rows = some_rows(at, self.rows_b)
+            term = self.parts[some_rows(self.at_a + at, self.rows_b), :] + self.recv_a[rows, :]
+            self.send_b[rows, :] = term.astype(BF16)
+            device = (2 * peer + ring.core, ring.space)
+            self.copies.append(
+                send(self.send_b.at[rows], self.recv_b.at[off], self.sems, off, device)
+            )
+        mine = some_rows(ring.chip * self.rows_b, self.rows_b)
+        self.own[...] = self.parts[some_rows(self.at_b, self.rows_b), :] + self.recv_a[mine, :]
+
+    def to_spaces(self):
+        ring = self.ring
+        self.wait()
+        self.copies = []
+        total = self.own[...]
+        for off in range(1, ring.chips):
+            total += self.recv_b[off].astype(F32)
+        self.own[...] = total
+        self.send_c[...] = total.astype(BF16)
+        for off in range(1, ring.spaces):
+            peer = ring.space_peer(off)
+            rows = some_rows(peer * self.rows_c, self.rows_c)
+            slot = ring.chips + off
+            self.copies.append(
+                send(self.send_c.at[rows], self.recv_c.at[off], self.sems, slot, (ring.member, peer))
+            )
+
+    def gather_spaces(self):
+        ring = self.ring
+        self.wait()
+        total = self.own[some_rows(ring.space * self.rows_c, self.rows_c), :]
+        for off in range(1, ring.spaces):
+            total += self.recv_c[off].astype(F32)
+        rows = some_rows(self.at_c, self.rows_c)
+        self.full[rows, :] = (total * self.scale).astype(BF16)
+        place = self.full.at[rows]
+        base = ring.chips + ring.spaces
+        self.copies = [
+            send(place, place, self.sems, base + off, (ring.member, ring.space_peer(off)))
+            for off in range(1, ring.spaces)
+        ]
+
+    def gather_chips(self):
+        ring = self.ring
+        self.wait()
+        place = self.full.at[some_rows(self.at_b, self.rows_b)]
+        base = ring.chips + 2 * ring.spaces
+        self.copies = [
+            send(
+                place, place, self.sems, base + off, (2 * ring.chip_peer(off) + ring.core, ring.space)
+            )
+            for off in range(1, ring.chips)
+        ]
+
+    def gather_cores(self):
+        ring = self.ring
+        self.wait()
+        place = self.full.at[some_rows(self.at_a, self.rows_a)]
+        slot = ring.chips + 2 * ring.spaces
+        self.copies = [send(place, place, self.sems, slot, (ring.sibling(), ring.space))]
+
+
+class Gains:
+    def __init__(self, ring, value, recv, sems):
+        self.ring, self.value, self.recv, self.sems = ring, value, recv, sems
+
+    @staticmethod
+    def scratch(width, chips, spaces):
+        return [
+            pltpu.VMEM((3, 8, width), F32),
+            pltpu.VMEM((chips + spaces, 8, width), F32),
+            pltpu.SemaphoreType.DMA((2, chips + spaces)),
+        ]
+
+    def peers(self, stage):
+        ring = self.ring
+        if stage == 0:
+            return [(0, (ring.sibling(), ring.space))]
+        if stage == 1:
+            return [
+                (off, (2 * ring.chip_peer(off) + ring.core, ring.space))
+                for off in range(1, ring.chips)
+            ]
+        return [
+            (ring.chips + off, (ring.member, ring.space_peer(off)))
+            for off in range(1, ring.spaces)
+        ]
+
+    def start(self, stage):
+        self.copies = [
+            send(self.value.at[stage], self.recv.at[slot], self.sems, slot, device)
+            for slot, device in self.peers(stage)
+        ]
+
+    def finish(self, stage):
+        for copy in self.copies:
+            copy.wait()
+        total = self.value[stage]
+        for slot, _ in self.peers(stage):
+            total += self.recv[slot]
+        return total
+
+
+def fetch_kernel(x_ref, og_ref, x_out, og_out, x_sems, og_sems, local):
+    ring = Ring()
+    ring.barrier(False)
+    moves = []
+    for i, (source, target, sems) in enumerate(
+        ((x_ref, x_out, x_sems), (og_ref, og_out, og_sems))
+    ):
+        move = Exchange(ring, source.shape[0], target.shape[1])
+        moves.append(move.start(source, target, sems, local.at[i], True))
+    for move in moves:
+        move.wait()
+
+
+def reduce_all(ring, pieces, gains, gains_ref, scale):
+    for piece in pieces:
+        piece.start()
+    gains.start(0)
+    for piece in pieces:
+        piece.to_chips()
+    gains.value[1] = gains.finish(0)
+    gains.start(1)
+    for piece in pieces:
+        piece.to_spaces()
+    gains.value[2] = gains.finish(1)
+    gains.start(2)
+    for piece in pieces:
+        piece.gather_spaces()
+    for piece in pieces:
+        piece.gather_chips()
+    for piece in pieces:
+        piece.gather_cores()
+    gains_ref[...] = gains.finish(2) * scale
+    for piece in pieces:
+        piece.wait()
+
+
+def share_kernel(scale, back_ref, wide_ref, square_ref, gain_ref, y_ref, wide_out, square_out,
+                 gains_out, *scratch):
+    ring = Ring()
+    ring.barrier(True)
+    y_sems, local = scratch[:2]
+    move = Exchange(ring, y_ref.shape[0], back_ref.shape[1])
+    pieces = [
+        Total(ring, scale, wide_ref, wide_out, *scratch[2:9]),
+        Total(ring, scale, square_ref, square_out, *scratch[9:16]),
+    ]
+    gains = Gains(ring, *scratch[16:19])
+    gains.value[0] = gain_ref[...]
+    move.start(back_ref, y_ref, y_sems, local.at[0], False)
+    reduce_all(ring, pieces, gains, gains_out, scale)
+    move.wait()
+
+
+def padded(rows, devices):
+    unit = 16 * devices
+    return -(-rows // unit) * unit
+
+
 def on_device(x, og, g1, wq, wk, wv, wo, g2, wu, wd):
-    groups = lax.axis_size("member")
+    groups, spaces = lax.axis_size("member"), lax.axis_size("space")
     own_members, own_patches, width = x.shape
     spread = own_patches // groups
     everyone = own_members * groups
     hidden = wu.shape[1]
     layer = Layer(everyone, spread, width, hidden)
-
-    def patchwise(array):
-        array = array.reshape(own_members, groups, spread, width)
-        array = lax.all_to_all(array, "member", split_axis=1, concat_axis=0, tiled=True)
-        return array.reshape(everyone, spread, width)
-
+    vmem = pl.BlockSpec(memory_space=pltpu.VMEM)
+    limit = 60 * 2**20
+    moved = jax.ShapeDtypeStruct((everyone, spread, width), BF16)
+    x_here, og_here = pl.pallas_call(
+        fetch_kernel,
+        out_shape=(moved, moved),
+        in_specs=[vmem] * 2,
+        out_specs=(vmem, vmem),
+        scratch_shapes=[
+            pltpu.SemaphoreType.DMA((2, groups)),
+            pltpu.SemaphoreType.DMA((2, groups)),
+            pltpu.SemaphoreType.DMA((2,)),
+        ],
+        compiler_params=pltpu.CompilerParams(
+            vmem_limit_bytes=limit, collective_id=0, has_side_effects=True
+        ),
+    )(x, og)
+    wide_rows = padded(2 * hidden, groups * spaces)
+    square_rows = padded(4 * width, groups * spaces)
     scratch = layer.scratch()
-    vmem = pl.BlockSpec(memory_space=pltpu.VMEM)
-    back, parts, gains = pl.pallas_call(
+    back, wide, square, gains = pl.pallas_call(
         functools.partial(kernel, layer, tuple(scratch)),
         out_shape=(
-            jax.ShapeDtypeStruct((everyone, spread, width), BF16),
-            jax.ShapeDtypeStruct((2 * hidden + 4 * width, width), F32),
-            jax.ShapeDtypeStruct((2, width), F32),
+            moved,
+            jax.ShapeDtypeStruct((wide_rows, width), F32),
+            jax.ShapeDtypeStruct((square_rows, width), F32),
+            jax.ShapeDtypeStruct((8, width), F32),
         ),
         in_specs=[vmem] * 10,
-        out_specs=(vmem, vmem, vmem),
+        out_specs=(vmem,) * 4,
         scratch_shapes=list(scratch.values()),
-        compiler_params=pltpu.CompilerParams(vmem_limit_bytes=60 * 2**20),
-    )(patchwise(x), patchwise(og), g1.reshape(1, width), wq, wk, wv, wo, g2.reshape(1, width), wu, wd)
-    back = lax.all_to_all(
-        back.reshape(everyone, 1, spread, width), "member", split_axis=0, concat_axis=1, tiled=True
-    ).reshape(own_members, own_patches, width)
+        compiler_params=pltpu.CompilerParams(vmem_limit_bytes=limit),
+    )(x_here, og_here, g1.reshape(1, width), wq, wk, wv, wo, g2.reshape(1, width), wu, wd)
+    scale = 1.0 / math.sqrt(everyone * own_patches * spaces)
+    chips = groups // 2
+    back, wide, square, gains = pl.pallas_call(
+        functools.partial(share_kernel, scale),
+        out_shape=(
+            jax.ShapeDtypeStruct(x.shape, BF16),
+            jax.ShapeDtypeStruct((wide_rows, width), BF16),
+            jax.ShapeDtypeStruct((square_rows, width), BF16),
+            jax.ShapeDtypeStruct((8, width), F32),
+        ),
+        in_specs=[vmem] * 4,
+        out_specs=(vmem,) * 4,
+        scratch_shapes=[
+            pltpu.SemaphoreType.DMA((2, groups)),
+            pltpu.SemaphoreType.DMA((1,)),
+            *Total.scratch(wide_rows, width, chips, spaces)[1:],
+            *Total.scratch(square_rows, width, chips, spaces)[1:],
+            *Gains.scratch(width, chips, spaces),
+        ],
+        compiler_params=pltpu.CompilerParams(
+            vmem_limit_bytes=limit, collective_id=1, has_side_effects=True
+        ),
+    )(back, wide, square, gains)
+    return finish(og, back, wide, square, gains, width, hidden)
+
+
+def finish(og, back, wide, square, gains, width, hidden):
     input_grad = og.astype(F32) + back.astype(F32)
-    scale = 1.0 / math.sqrt(everyone * own_patches * lax.axis_size("space"))
-    parts, gains = lax.psum((parts, gains), ("member", "space"))
-    return finish(input_grad, parts * scale, gains * scale, width, hidden)
-
-
-def finish(input_grad, parts, gains, width, hidden):
-    down = parts[:hidden]
-    up = parts[hidden : 2 * hidden].reshape(hidden // width, width, width)
+    wide, square = wide.astype(F32), square.astype(F32)
+    up = wide[hidden : 2 * hidden].reshape(hidden // width, width, width)
     up = up.transpose(1, 0, 2).reshape(width, hidden)
-    squares = [parts[2 * hidden + width * i : 2 * hidden + width * (i + 1)] for i in range(4)]
-    return (input_grad, *squares, up, down, gains[0], gains[1])
+    squares = [square[width * i : width * (i + 1)] for i in range(4)]
+    return (input_grad, *squares, up, wide[:hidden], gains[0], gains[1])
 
 
 def solution(mesh):

time: 218 us -> 96 us (0.44)
  waiting for transfers between devices: 95.7 us -> 0 us
  blocking collectives: 60.1 us -> 0 us
  Pallas kernels: 29 us -> 88.4 us
  between operations: 14.1 us -> 0.67 us
  starting transfers between devices: 8.84 us -> 0 us
  local copies, waits for them, and re-layouts: 6.8 us -> 4.57 us
    psum x1 -> x0, waiting for transfers between devices: 87.1 us -> none  [on_device(): parts, gains = lax.psum((parts, gains), ('member', 'space'))]
    pallas_call x0 -> x2, Pallas kernels: none -> 60 us  [the longest x1 41.7 us: on_device(): pl.pallas_call(functools.partial(share_kernel, scale), out_shape=(jax.Sha...]
    psum x1 -> x0, blocking collectives: 47.2 us -> none  [on_device(): parts, gains = lax.psum((parts, gains), ('member', 'space'))]
    all_to_all x1 -> x0, blocking collectives: 12.8 us -> none  [patchwise(): lax.all_to_all(array, 'member', split_axis=1, concat_axis=0, tiled=True)]
    all_to_all x2 -> x0, starting transfers between devices: 8.81 us -> none  [the longest x1 5.17 us: patchwise(): lax.all_to_all(array, 'member', split_axis=1, concat_axis=0, tiled=True)]
    all_to_all x2 -> x0, waiting for transfers between devices: 8.62 us -> none  [the longest x1 8.62 us: patchwise(): lax.all_to_all(array, 'member', split_axis=1, concat_axis=0, tiled=True)]
    reshape x2 -> x0, local copies, waits for them, and re-layouts: 2.95 us -> none  [patchwise(): array = array.reshape(own_members, groups, spread, width)]
  transfers between devices with their start and end apart: 3 -> 0, of which waited for: 2 -> 0; matrix products, arithmetic and copies ran while one was open for 1% -> 0% of each run, Pallas kernels for 0% -> 0%
where the time goes in v2:
time: 96 us; the launch traced here: 95.8 us
  Pallas kernels  88.4 us (92%)
  local copies, waits for them, and re-layouts  4.57 us (5%)
  other arithmetic  2.21 us (2%)
    pallas_call x1, Pallas kernels, on_device(): pl.pallas_call(functools.partial(share_kernel, scale), out_shape=(jax.Sha...  41.7 us
    pallas_call x1, Pallas kernels, on_device(): pl.pallas_call(functools.partial(kernel, layer, tuple(scratch)), out_shap...  28.3 us
    pallas_call x1, Pallas kernels, on_device(): pl.pallas_call(fetch_kernel, out_shape=(moved, moved), in_specs=[vmem] *...  18.4 us
    slice x2, local copies, waits for them, and re-layouts, finish(): return (input_grad, *squares, up, wide[:hidden], gains[0], gains[1])  2.47 us
    add x1, other arithmetic, finish(): input_grad = og.astype(F32) + back.astype(F32)  2.21 us

profile of v2, /device:TPU:0, one launch (start us, length us, event | category | flops | bytes accessed | tf_op | source)
XLA Modules:
  0.0 95.8 jit_solution(17439830978643003225)
XLA Ops:
  0.6 18.4 %shard_map.169 = (bf16[32,32,256]{2,1,0:T(8,128)(2,1)}, bf16[32,32,256]{2,1,0:T(8,128)(2,1)}) custom-call(bf16[4,256,256]{2,1,0:T(8,128)(2,1)} %x_ref.1, bf16[4,256,256]{2,1,0:T(8,128)(2,1)} %og_ref.1), custom_call_target="tpu_custom_call" | custom-call | tf_op jit(solution)/shard_map/pallas_call | solution.py:526
  19.0 28.3 %shard_map.170 = (bf16[32,32,256]{2,1,0:T(8,128)(2,1)}, f32[2048,256]{1,0:T(8,128)}, f32[1024,256]{1,0:T(8,128)}, f32[8,256]{1,0:T(8,128)}) custom-call(bf16[32,32,256]{2,1,0:T(8,128)(2,1)} %get-tuple-element.19.refs_0_, bf16[32,32,256]{2,1,0:T(8,128)(2,1)} %get-tuple-element.20.refs_1_, f32[1,256]{1,0:T(1,128)} %bitcast.11, bf16[256,256]{1,0:T(8,128)(2,1)} %refs_3_.1, ...), custom_call_target="tpu_custom_call" | custom-call | tf_op jit(solution)/shard_map/pallas_call | solution.py:543
  47.4 0.0 copy-start.2
  47.4 41.7 %shard_map.171 = (bf16[4,256,256]{2,1,0:T(8,128)(2,1)}, bf16[2048,256]{1,0:T(8,128)(2,1)}, bf16[1024,256]{1,0:T(8,128)(2,1)}, f32[8,256]{1,0:T(8,128)}) custom-call(bf16[32,32,256]{2,1,0:T(8,128)(2,1)} %get-tuple-element.21.back_ref, f32[2048,256]{1,0:T(8,128)} %get-tuple-element.22.wide_ref, f32[1024,256]{1,0:T(8,128)} %get-tuple-element.23.square_ref, ...), custom_call_target="tpu_custom_call" | custom-call | tf_op jit(solution)/shard_map/pallas_call | solution.py:558
  89.0 0.0 copy-start.1
  89.0 1.3 %fusion.2 = (f32[1,256]{1,0:T(1,128)}, f32[1,256]{1,0:T(1,128)}) fusion(f32[8,256]{1,0:T(8,128)} %get-tuple-element.28), kind=kLoop, calls=%fused_computation.3 | loop fusion | bytes 4096 | tf_op jit(solution)/shard_map/slice | solution.py:588
  90.4 0.0 copy-done.2
  90.4 0.0 copy-start
  90.4 2.2 %convert_add_fusion = f32[4,256,256]{2,1,0:T(8,128)} fusion(bf16[4,256,256]{2,1,0:T(8,128)(2,1)} %get-tuple-element.25, bf16[4,256,256]{2,1,0:T(8,128)(2,1)S(1)} %copy-done.2), kind=kLoop, calls=%fused_computation | loop fusion | flops 786432 | bytes 2097152 | tf_op jit(solution)/shard_map/add | solution.py:583
  92.6 0.0 copy-done.1
  92.6 1.0 %fusion.1 = (f32[256,256]{1,0:T(8,128)}, f32[256,256]{1,0:T(8,128)}, f32[256,256]{1,0:T(8,128)}, f32[256,256]{1,0:T(8,128)}) fusion(bf16[1024,256]{1,0:T(8,128)(2,1)S(1)} %copy-done.1), kind=kLoop, calls=%fused_computation.2 | loop fusion | bytes 2097152 | tf_op jit(solution)/shard_map/slice | solution.py:587
  93.6 0.0 copy-done
  93.6 1.1 %fusion = (f32[1024,256]{1,0:T(8,128)}, f32[1024,256]{1,0:T(8,128)S(1)}) fusion(bf16[2048,256]{1,0:T(8,128)(2,1)S(1)} %copy-done), kind=kLoop, calls=%fused_computation.1 | loop fusion | bytes 4194304 | tf_op jit(solution)/shard_map/slice | solution.py:588
  94.7 1.1 %copy.20 = f32[4,32,8,256]{3,2,0,1:T(8,128)} copy(f32[4,32,8,256]{3,2,1,0:T(8,128)S(1)} %bitcast.9) | data formatting | bytes 2097152 | tf_op jit(solution)/shard_map/reshape | solution.py:586
Async XLA Ops:
  47.4 43.0 %copy-start.2 = (bf16[4,256,256]{2,1,0:T(8,128)(2,1)S(1)}, bf16[4,256,256]{2,1,0:T(8,128)(2,1)}, u32[]{:S(2)}) copy-start(bf16[4,256,256]{2,1,0:T(8,128)(2,1)} %og_ref.1) | copy-start | bytes 1572868
  89.0 3.6 %copy-start.1 = (bf16[1024,256]{1,0:T(8,128)(2,1)S(1)}, bf16[1024,256]{1,0:T(8,128)(2,1)}, u32[]{:S(2)}) copy-start(bf16[1024,256]{1,0:T(8,128)(2,1)} %get-tuple-element.26) | copy-start | bytes 1572868
  90.4 3.2 %copy-start = (bf16[2048,256]{1,0:T(8,128)(2,1)S(1)}, bf16[2048,256]{1,0:T(8,128)(2,1)}, u32[]{:S(2)}) copy-start(bf16[2048,256]{1,0:T(8,128)(2,1)} %get-tuple-element.27) | copy-start | bytes 3145732

commit v3 on v2

--- a/solution.py
+++ b/solution.py
@@ -72,9 +72,6 @@
             ga=pltpu.VMEM((groups, rows, width), BF16),
             gm=pltpu.VMEM((groups, rows, width), BF16),
             gh=pltpu.VMEM((groups, rows, width), F32),
-            gq=pltpu.VMEM((groups, rows, width), BF16),
-            gk=pltpu.VMEM((groups, rows, width), BF16),
-            gv=pltpu.VMEM((groups, rows, width), BF16),
             p=pltpu.VMEM((groups, self.heads, rows, rows), F32),
         )
 
@@ -160,7 +157,7 @@
             grad_q += dot(dscore, keys * mask)
             grad_k += dot_tn(dscore, query * mask)
         grad_q, grad_k, grad_v = (grad.astype(BF16) for grad in (grad_q, grad_k, grad_v))
-        s["gq"][g], s["gk"][g], s["gv"][g] = grad_q, grad_k, grad_v
+        s["q"][g], s["k"][g], s["v"][g] = grad_q, grad_k, grad_v
         grad_normed = (
             dot_nt(grad_q, w["wq"][...])
             + dot_nt(grad_k, w["wk"][...])
@@ -188,7 +185,7 @@
     def square_parts(self, s, parts):
         normed = self.flat(s, "n1")
         at = 0
-        for name in ("gq", "gk", "gv"):
+        for name in ("q", "k", "v"):
             parts[at : at + self.width, :] = dot_tn(normed, self.flat(s, name))
             at += self.width
         parts[at : at + self.width, :] = dot_tn(self.flat(s, "mix"), self.flat(s, "ga"))
@@ -201,29 +198,6 @@
 
 
 WEIGHTS = ("g1", "wq", "wk", "wv", "wo", "g2", "wu", "wd")
-
-
-def kernel(layer, names, *refs):
-    x_ref, og_ref = refs[:2]
-    w = dict(zip(WEIGHTS, refs[2:10]))
-    y_ref, wide_ref, square_ref, gains_ref = refs[10:14]
-    s = dict(zip(names, refs[14:]))
-    layer.regroup(x_ref, s["x"])
-    layer.regroup(og_ref, s["og"])
-    zero = jnp.zeros((1, layer.width), F32)
-
-    @pl.loop(0, layer.groups)
-    def _(g):
-        layer.attention(s, w, g)
-
-    gain2 = lax.fori_loop(0, layer.groups, lambda g, c: layer.feed_forward(s, w, g, c), zero)
-    layer.wide_parts(s, wide_ref)
-    gain1 = lax.fori_loop(0, layer.groups, lambda g, c: layer.attention_back(s, w, g, c), zero)
-    layer.square_parts(s, square_ref)
-    layer.ungroup(s["gh"], y_ref)
-    gains_ref[...] = jnp.zeros_like(gains_ref)
-    gains_ref[0:1, :] = gain1
-    gains_ref[1:2, :] = gain2
 
 
 class Ring:
@@ -318,18 +292,17 @@
         self.at_c = self.at_b + ring.space * self.rows_c
 
     @staticmethod
-    def scratch(rows, width, chips, spaces):
+    def scratch(rows, width, chips, spaces, held):
         a = rows // 2
         b = a // chips
         c = b // spaces
         slots = 2 * (chips + spaces)
         return [
-            pltpu.VMEM((rows, width), BF16),
             pltpu.VMEM((a, width), F32),
-            pltpu.VMEM((a, width), BF16),
-            pltpu.VMEM((chips, b, width), BF16),
-            pltpu.VMEM((b, width), BF16),
-            pltpu.VMEM((spaces, c, width), BF16),
+            pltpu.VMEM((a, width), held),
+            pltpu.VMEM((chips, b, width), held),
+            pltpu.VMEM((b, width), held),
+            pltpu.VMEM((spaces, c, width), held),
             pltpu.VMEM((b, width), F32),
             pltpu.SemaphoreType.DMA((2, slots)),
         ]
@@ -354,7 +327,7 @@
             at = peer * self.rows_b
             rows = some_rows(at, self.rows_b)
             term = self.parts[some_rows(self.at_a + at, self.rows_b), :] + self.recv_a[rows, :]
-            self.send_b[rows, :] = term.astype(BF16)
+            self.send_b[rows, :] = term.astype(self.send_b.dtype)
             device = (2 * peer + ring.core, ring.space)
             self.copies.append(
                 send(self.send_b.at[rows], self.recv_b.at[off], self.sems, off, device)
@@ -370,7 +343,7 @@
         for off in range(1, ring.chips):
             total += self.recv_b[off].astype(F32)
         self.own[...] = total
-        self.send_c[...] = total.astype(BF16)
+        self.send_c[...] = total.astype(self.send_c.dtype)
         for off in range(1, ring.spaces):
             peer = ring.space_peer(off)
             rows = some_rows(peer * self.rows_c, self.rows_c)
@@ -455,57 +428,66 @@
         return total
 
 
-def fetch_kernel(x_ref, og_ref, x_out, og_out, x_sems, og_sems, local):
+def kernel(layer, scale, names, *refs):
+    x_ref, og_ref = refs[:2]
+    w = dict(zip(WEIGHTS, refs[2:10]))
+    y_ref, wide_out, square_out, gains_out = refs[10:14]
+    s = dict(zip(names, refs[14:]))
+    rest = refs[14 + len(names) :]
+    x_here, og_here, x_sems, og_sems, y_sems, local, wide_ref, square_ref = rest[:8]
     ring = Ring()
-    ring.barrier(False)
-    moves = []
-    for i, (source, target, sems) in enumerate(
-        ((x_ref, x_out, x_sems), (og_ref, og_out, og_sems))
-    ):
-        move = Exchange(ring, source.shape[0], target.shape[1])
-        moves.append(move.start(source, target, sems, local.at[i], True))
-    for move in moves:
-        move.wait()
-
-
-def reduce_all(ring, pieces, gains, gains_ref, scale):
-    for piece in pieces:
-        piece.start()
+    wide = Total(ring, scale, wide_ref, wide_out, *rest[8:15])
+    square = Total(ring, scale, square_ref, square_out, *rest[15:22])
+    gains = Gains(ring, *rest[22:25])
+    own, spread = x_ref.shape[0], layer.patches
+    x_move, og_move, y_move = (Exchange(ring, own, spread) for _ in range(3))
+
+    ring.barrier(True)
+    x_move.start(x_ref, x_here, x_sems, local.at[0], True)
+    og_move.start(og_ref, og_here, og_sems, local.at[1], True)
+    x_move.wait()
+    layer.regroup(x_here, s["x"])
+
+    @pl.loop(0, layer.groups)
+    def _(g):
+        layer.attention(s, w, g)
+
+    og_move.wait()
+    layer.regroup(og_here, s["og"])
+    zero = jnp.zeros((1, layer.width), F32)
+    gain2 = lax.fori_loop(0, layer.groups, lambda g, c: layer.feed_forward(s, w, g, c), zero)
+    layer.wide_parts(s, wide_ref)
+    wide.start()
+    first = max(1, layer.groups // 4)
+    back = functools.partial(layer.attention_back, s, w)
+    gain1 = lax.fori_loop(0, first, back, zero)
+    wide.to_chips()
+    gain1 = lax.fori_loop(first, layer.groups, back, gain1)
+    layer.square_parts(s, square_ref)
+    square.start()
+    gains.value[0] = jnp.zeros_like(gains.value[0])
+    gains.value[0, 0:1, :] = gain1
+    gains.value[0, 1:2, :] = gain2
     gains.start(0)
-    for piece in pieces:
-        piece.to_chips()
+    layer.ungroup(s["gh"], x_here)
+    wide.to_spaces()
+    square.to_chips()
+    y_move.start(x_here, y_ref, y_sems, local.at[2], False)
     gains.value[1] = gains.finish(0)
     gains.start(1)
-    for piece in pieces:
-        piece.to_spaces()
+    wide.gather_spaces()
+    square.to_spaces()
     gains.value[2] = gains.finish(1)
     gains.start(2)
-    for piece in pieces:
-        piece.gather_spaces()
-    for piece in pieces:
-        piece.gather_chips()
-    for piece in pieces:
-        piece.gather_cores()
-    gains_ref[...] = gains.finish(2) * scale
-    for piece in pieces:
-        piece.wait()
-
-
-def share_kernel(scale, back_ref, wide_ref, square_ref, gain_ref, y_ref, wide_out, square_out,
-                 gains_out, *scratch):
-    ring = Ring()
-    ring.barrier(True)
-    y_sems, local = scratch[:2]
-    move = Exchange(ring, y_ref.shape[0], back_ref.shape[1])
-    pieces = [
-        Total(ring, scale, wide_ref, wide_out, *scratch[2:9]),
-        Total(ring, scale, square_ref, square_out, *scratch[9:16]),
-    ]
-    gains = Gains(ring, *scratch[16:19])
-    gains.value[0] = gain_ref[...]
-    move.start(back_ref, y_ref, y_sems, local.at[0], False)
-    reduce_all(ring, pieces, gains, gains_out, scale)
-    move.wait()
+    wide.gather_chips()
+    square.gather_spaces()
+    wide.gather_cores()
+    square.gather_chips()
+    gains_out[...] = gains.finish(2) * scale
+    square.gather_cores()
+    y_move.wait()
+    wide.wait()
+    square.wait()
 
 
 def padded(rows, devices):
@@ -521,61 +503,37 @@
     hidden = wu.shape[1]
     layer = Layer(everyone, spread, width, hidden)
     vmem = pl.BlockSpec(memory_space=pltpu.VMEM)
-    limit = 60 * 2**20
-    moved = jax.ShapeDtypeStruct((everyone, spread, width), BF16)
-    x_here, og_here = pl.pallas_call(
-        fetch_kernel,
-        out_shape=(moved, moved),
-        in_specs=[vmem] * 2,
-        out_specs=(vmem, vmem),
-        scratch_shapes=[
-            pltpu.SemaphoreType.DMA((2, groups)),
-            pltpu.SemaphoreType.DMA((2, groups)),
-            pltpu.SemaphoreType.DMA((2,)),
-        ],
-        compiler_params=pltpu.CompilerParams(
-            vmem_limit_bytes=limit, collective_id=0, has_side_effects=True
-        ),
-    )(x, og)
+    limit = 62 * 2**20
     wide_rows = padded(2 * hidden, groups * spaces)
     square_rows = padded(4 * width, groups * spaces)
+    chips = groups // 2
+    scale = 1.0 / math.sqrt(everyone * own_patches * spaces)
     scratch = layer.scratch()
     back, wide, square, gains = pl.pallas_call(
-        functools.partial(kernel, layer, tuple(scratch)),
-        out_shape=(
-            moved,
-            jax.ShapeDtypeStruct((wide_rows, width), F32),
-            jax.ShapeDtypeStruct((square_rows, width), F32),
-            jax.ShapeDtypeStruct((8, width), F32),
-        ),
-        in_specs=[vmem] * 10,
-        out_specs=(vmem,) * 4,
-        scratch_shapes=list(scratch.values()),
-        compiler_params=pltpu.CompilerParams(vmem_limit_bytes=limit),
-    )(x_here, og_here, g1.reshape(1, width), wq, wk, wv, wo, g2.reshape(1, width), wu, wd)
-    scale = 1.0 / math.sqrt(everyone * own_patches * spaces)
-    chips = groups // 2
-    back, wide, square, gains = pl.pallas_call(
-        functools.partial(share_kernel, scale),
+        functools.partial(kernel, layer, scale, tuple(scratch)),
         out_shape=(
             jax.ShapeDtypeStruct(x.shape, BF16),
             jax.ShapeDtypeStruct((wide_rows, width), BF16),
             jax.ShapeDtypeStruct((square_rows, width), BF16),
             jax.ShapeDtypeStruct((8, width), F32),
         ),
-        in_specs=[vmem] * 4,
+        in_specs=[vmem] * 10,
         out_specs=(vmem,) * 4,
         scratch_shapes=[
-            pltpu.SemaphoreType.DMA((2, groups)),
-            pltpu.SemaphoreType.DMA((1,)),
-            *Total.scratch(wide_rows, width, chips, spaces)[1:],
-            *Total.scratch(square_rows, width, chips, spaces)[1:],
+            *scratch.values(),
+            *[pltpu.VMEM((everyone, spread, width), BF16)] * 2,
+            *[pltpu.SemaphoreType.DMA((2, groups))] * 3,
+            pltpu.SemaphoreType.DMA((3,)),
+            pltpu.VMEM((wide_rows, width), F32),
+            pltpu.VMEM((square_rows, width), F32),
+            *Total.scratch(wide_rows, width, chips, spaces, BF16),
+            *Total.scratch(square_rows, width, chips, spaces, F32),
             *Gains.scratch(width, chips, spaces),
         ],
         compiler_params=pltpu.CompilerParams(
-            vmem_limit_bytes=limit, collective_id=1, has_side_effects=True
+            vmem_limit_bytes=limit, collective_id=0, has_side_effects=True
         ),
-    )(back, wide, square, gains)
+    )(x, og, g1.reshape(1, width), wq, wk, wv, wo, g2.reshape(1, width), wu, wd)
     return finish(og, back, wide, square, gains, width, hidden)
 
 

time: 96 us -> 80.5 us (0.84)
  Pallas kernels: 88.4 us -> 72.8 us
  local copies, waits for them, and re-layouts: 4.57 us -> 5.76 us
  other arithmetic: 2.21 us -> 1.08 us
    pallas_call x3 -> x1, Pallas kernels: 88.4 us -> 72.8 us  [on_device(): pl.pallas_call(functools.partial(kernel, layer, scale, tuple(scratch)), o...]
    slice x1, local copies, waits for them, and re-layouts: 0.98 us -> 2.16 us  [finish(): squares = [square[width * i:width * (i + 1)] for i in range(4)]]
    add x1, other arithmetic: 2.21 us -> 1.08 us  [finish(): input_grad = og.astype(F32) + back.astype(F32)]
where the time goes in v3:
time: 80.5 us; the launch traced here: 80.3 us
  Pallas kernels  72.8 us (90%)
  local copies, waits for them, and re-layouts  5.76 us (7%)
  other arithmetic  1.08 us (1%)
    pallas_call x1, Pallas kernels, on_device(): pl.pallas_call(functools.partial(kernel, layer, scale, tuple(scratch)), o...  72.8 us
    slice x2, local copies, waits for them, and re-layouts, finish(): return (input_grad, *squares, up, wide[:hidden], gains[0], gains[1])  2.47 us
    slice x1, local copies, waits for them, and re-layouts, finish(): squares = [square[width * i:width * (i + 1)] for i in range(4)]  2.16 us

profile of v3, /device:TPU:0, one launch (start us, length us, event | category | flops | bytes accessed | tf_op | source)
XLA Modules:
  0.0 80.3 jit_solution(9916934232747934974)
XLA Ops:
  0.6 72.8 %shard_map.169 = (bf16[4,256,256]{2,1,0:T(8,128)(2,1)}, bf16[2048,256]{1,0:T(8,128)(2,1)}, bf16[1024,256]{1,0:T(8,128)(2,1)}, f32[8,256]{1,0:T(8,128)}) custom-call(bf16[4,256,256]{2,1,0:T(8,128)(2,1)} %refs_0_.1, bf16[4,256,256]{2,1,0:T(8,128)(2,1)} %refs_1_.1, f32[1,256]{1,0:T(1,128)} %bitcast.11, bf16[256,256]{1,0:T(8,128)(2,1)} %refs_3_.1, ...), custom_call_target="tpu_custom_call" | custom-call | tf_op jit(solution)/shard_map/pallas_call | solution.py:512
  73.4 0.0 copy-start
  73.5 2.2 %fusion.1 = (f32[256,256]{1,0:T(8,128)}, f32[256,256]{1,0:T(8,128)}, f32[256,256]{1,0:T(8,128)}, f32[256,256]{1,0:T(8,128)}) fusion(bf16[1024,256]{1,0:T(8,128)(2,1)} %get-tuple-element.14), kind=kLoop, calls=%fused_computation.2 | loop fusion | bytes 2097152 | tf_op jit(solution)/shard_map/slice | solution.py:545
  75.6 0.0 copy-done
  75.6 1.1 %fusion = (f32[1024,256]{1,0:T(8,128)}, f32[1024,256]{1,0:T(8,128)S(1)}) fusion(bf16[2048,256]{1,0:T(8,128)(2,1)S(1)} %copy-done), kind=kLoop, calls=%fused_computation.1 | loop fusion | bytes 4194304 | tf_op jit(solution)/shard_map/slice | solution.py:546
  76.8 0.0 copy-start.1
  76.8 0.0 copy-start.2
  76.8 1.1 %copy.20 = f32[4,32,8,256]{3,2,0,1:T(8,128)} copy(f32[4,32,8,256]{3,2,1,0:T(8,128)S(1)} %bitcast.9) | data formatting | bytes 2097152 | tf_op jit(solution)/shard_map/reshape | solution.py:544
  77.9 1.3 %fusion.2 = (f32[1,256]{1,0:T(1,128)}, f32[1,256]{1,0:T(1,128)}) fusion(f32[8,256]{1,0:T(8,128)} %get-tuple-element.16), kind=kLoop, calls=%fused_computation.3 | loop fusion | bytes 4096 | tf_op jit(solution)/shard_map/slice | solution.py:546
  79.2 0.0 copy-done.1
  79.2 0.0 copy-done.2
  79.2 1.1 %convert_add_fusion = f32[4,256,256]{2,1,0:T(8,128)} fusion(bf16[4,256,256]{2,1,0:T(8,128)(2,1)S(1)} %copy-done.2, bf16[4,256,256]{2,1,0:T(8,128)(2,1)S(1)} %copy-done.1), kind=kLoop, calls=%fused_computation | loop fusion | flops 786432 | bytes 2097152 | tf_op jit(solution)/shard_map/add | solution.py:541
Async XLA Ops:
  73.4 2.2 %copy-start = (bf16[2048,256]{1,0:T(8,128)(2,1)S(1)}, bf16[2048,256]{1,0:T(8,128)(2,1)}, u32[]{:S(2)}) copy-start(bf16[2048,256]{1,0:T(8,128)(2,1)} %get-tuple-element.15) | copy-start | bytes 3145732
  76.8 2.5 %copy-start.1 = (bf16[4,256,256]{2,1,0:T(8,128)(2,1)S(1)}, bf16[4,256,256]{2,1,0:T(8,128)(2,1)}, u32[]{:S(2)}) copy-start(bf16[4,256,256]{2,1,0:T(8,128)(2,1)} %refs_1_.1) | copy-start | bytes 1572868
  76.8 2.5 %copy-start.2 = (bf16[4,256,256]{2,1,0:T(8,128)(2,1)S(1)}, bf16[4,256,256]{2,1,0:T(8,128)(2,1)}, u32[]{:S(2)}) copy-start(bf16[4,256,256]{2,1,0:T(8,128)(2,1)} %get-tuple-element.13) | copy-start | bytes 1572868

commit v4 on v3

--- a/solution.py
+++ b/solution.py
@@ -80,21 +80,17 @@
         inside = (lanes >= head * HEAD_DIM) & (lanes < (head + 1) * HEAD_DIM)
         return jnp.where(inside, 1.0, 0.0).astype(BF16)
 
-    def regroup(self, source, target):
-        for pair in range(self.groups // 2):
-            block = source[:, 16 * pair : 16 * pair + 16, :].astype(F32)
-            for half in range(2):
-                piece = block[:, 8 * half : 8 * half + 8, :].reshape(self.rows, self.width)
-                target[2 * pair + half] = piece.astype(target.dtype)
-
-    def ungroup(self, source, target):
-        for pair in range(self.groups // 2):
-            halves = [
-                source[2 * pair + half].reshape(self.members, 8, self.width) for half in range(2)
-            ]
-            target[:, 16 * pair : 16 * pair + 16, :] = jnp.concatenate(halves, axis=1).astype(
-                target.dtype
-            )
+    def regroup(self, pair, source, target):
+        block = source[:, 16 * pair : 16 * pair + 16, :].astype(F32)
+        for half in range(2):
+            piece = block[:, 8 * half : 8 * half + 8, :].reshape(self.rows, self.width)
+            target[2 * pair + half] = piece.astype(target.dtype)
+
+    def ungroup(self, pair, source, target):
+        halves = [source[2 * pair + half].reshape(self.members, 8, self.width) for half in range(2)]
+        target[:, 16 * pair : 16 * pair + 16, :] = jnp.concatenate(halves, axis=1).astype(
+            target.dtype
+        )
 
     def attention(self, s, w, g):
         unit, _ = norm_rows(s["x"][g])
@@ -250,14 +246,14 @@
 
 
 class Exchange:
-    def __init__(self, ring, own, spread):
-        self.ring, self.own, self.spread = ring, own, spread
+    def __init__(self, ring, own, spread, pair):
+        self.ring, self.own, self.spread, self.pair = ring, own, spread, pair
 
     def mine(self, ref, index):
-        return ref.at[:, some_rows(index * self.spread, self.spread), :]
+        return ref.at[:, some_rows(index * self.spread + 16 * self.pair, 16), :]
 
     def here(self, ref, index):
-        return ref.at[pl.ds(index * self.own, self.own), :, :]
+        return ref.at[pl.ds(index * self.own, self.own), pl.ds(16 * self.pair, 16), :]
 
     def start(self, source, target, sems, local, to_patch):
         ring = self.ring
@@ -266,9 +262,17 @@
         for off in range(1, ring.members):
             peer = ring.member_peer(off)
             self.copies.append(
-                send(take(source, peer), put(target, ring.member), sems, off, (peer, ring.space))
+                send(
+                    take(source, peer),
+                    put(target, ring.member),
+                    sems.at[self.pair],
+                    off,
+                    (peer, ring.space),
+                )
             )
-        own = pltpu.make_async_copy(take(source, ring.member), put(target, ring.member), local)
+        own = pltpu.make_async_copy(
+            take(source, ring.member), put(target, ring.member), local.at[self.pair]
+        )
         own.start()
         self.copies.append(own)
         return self
@@ -279,11 +283,10 @@
 
 
 class Total:
-    def __init__(self, ring, scale, parts, full, recv_a, send_b, recv_b, send_c, recv_c, own, sems):
+    def __init__(self, ring, scale, parts, full, recv_a, recv_b, recv_c, own, sems):
         self.ring, self.scale = ring, scale
         self.parts, self.full, self.sems, self.own = parts, full, sems, own
-        self.recv_a, self.send_b, self.recv_b = recv_a, send_b, recv_b
-        self.send_c, self.recv_c = send_c, recv_c
+        self.recv_a, self.recv_b, self.recv_c = recv_a, recv_b, recv_c
         self.rows_a = parts.shape[0] // 2
         self.rows_b = self.rows_a // ring.chips
         self.rows_c = self.rows_b // ring.spaces
@@ -292,17 +295,15 @@
         self.at_c = self.at_b + ring.space * self.rows_c
 
     @staticmethod
-    def scratch(rows, width, chips, spaces, held):
+    def scratch(rows, width, chips, spaces):
         a = rows // 2
         b = a // chips
         c = b // spaces
         slots = 2 * (chips + spaces)
         return [
             pltpu.VMEM((a, width), F32),
-            pltpu.VMEM((a, width), held),
-            pltpu.VMEM((chips, b, width), held),
-            pltpu.VMEM((b, width), held),
-            pltpu.VMEM((spaces, c, width), held),
+            pltpu.VMEM((chips, b, width), F32),
+            pltpu.VMEM((spaces, c, width), F32),
             pltpu.VMEM((b, width), F32),
             pltpu.SemaphoreType.DMA((2, slots)),
         ]
@@ -326,11 +327,11 @@
             peer = ring.chip_peer(off)
             at = peer * self.rows_b
             rows = some_rows(at, self.rows_b)
-            term = self.parts[some_rows(self.at_a + at, self.rows_b), :] + self.recv_a[rows, :]
-            self.send_b[rows, :] = term.astype(self.send_b.dtype)
+            place = some_rows(self.at_a + at, self.rows_b)
+            self.parts[place, :] = self.parts[place, :] + self.recv_a[rows, :]
             device = (2 * peer + ring.core, ring.space)
             self.copies.append(
-                send(self.send_b.at[rows], self.recv_b.at[off], self.sems, off, device)
+                send(self.parts.at[place], self.recv_b.at[off], self.sems, off, device)
             )
         mine = some_rows(ring.chip * self.rows_b, self.rows_b)
         self.own[...] = self.parts[some_rows(self.at_b, self.rows_b), :] + self.recv_a[mine, :]
@@ -341,15 +342,14 @@
         self.copies = []
         total = self.own[...]
         for off in range(1, ring.chips):
-            total += self.recv_b[off].astype(F32)
+            total += self.recv_b[off]
         self.own[...] = total
-        self.send_c[...] = total.astype(self.send_c.dtype)
         for off in range(1, ring.spaces):
             peer = ring.space_peer(off)
             rows = some_rows(peer * self.rows_c, self.rows_c)
             slot = ring.chips + off
             self.copies.append(
-                send(self.send_c.at[rows], self.recv_c.at[off], self.sems, slot, (ring.member, peer))
+                send(self.own.at[rows], self.recv_c.at[off], self.sems, slot, (ring.member, peer))
             )
 
     def gather_spaces(self):
@@ -357,7 +357,7 @@
         self.wait()
         total = self.own[some_rows(ring.space * self.rows_c, self.rows_c), :]
         for off in range(1, ring.spaces):
-            total += self.recv_c[off].astype(F32)
+            total += self.recv_c[off]
         rows = some_rows(self.at_c, self.rows_c)
         self.full[rows, :] = (total * self.scale).astype(BF16)
         place = self.full.at[rows]
@@ -436,56 +436,66 @@
     rest = refs[14 + len(names) :]
     x_here, og_here, x_sems, og_sems, y_sems, local, wide_ref, square_ref = rest[:8]
     ring = Ring()
-    wide = Total(ring, scale, wide_ref, wide_out, *rest[8:15])
-    square = Total(ring, scale, square_ref, square_out, *rest[15:22])
-    gains = Gains(ring, *rest[22:25])
+    wide = Total(ring, scale, wide_ref, wide_out, *rest[8:13])
+    square = Total(ring, scale, square_ref, square_out, *rest[13:18])
+    gains = Gains(ring, *rest[18:21])
     own, spread = x_ref.shape[0], layer.patches
-    x_move, og_move, y_move = (Exchange(ring, own, spread) for _ in range(3))
+    pairs = layer.groups // 2
+    x_moves, og_moves, y_moves = (
+        [Exchange(ring, own, spread, pair) for pair in range(pairs)] for _ in range(3)
+    )
 
     ring.barrier(True)
-    x_move.start(x_ref, x_here, x_sems, local.at[0], True)
-    og_move.start(og_ref, og_here, og_sems, local.at[1], True)
-    x_move.wait()
-    layer.regroup(x_here, s["x"])
-
-    @pl.loop(0, layer.groups)
-    def _(g):
-        layer.attention(s, w, g)
-
-    og_move.wait()
-    layer.regroup(og_here, s["og"])
+    for move in x_moves:
+        move.start(x_ref, x_here, x_sems, local.at[0], True)
+    for pair in range(pairs):
+        x_moves[pair].wait()
+        og_moves[pair].start(og_ref, og_here, og_sems, local.at[1], True)
+        layer.regroup(pair, x_here, s["x"])
+
+        @pl.loop(2 * pair, 2 * pair + 2)
+        def _(g):
+            layer.attention(s, w, g)
+
     zero = jnp.zeros((1, layer.width), F32)
-    gain2 = lax.fori_loop(0, layer.groups, lambda g, c: layer.feed_forward(s, w, g, c), zero)
+    gain1 = gain2 = zero
+    for pair in range(pairs):
+        og_moves[pair].wait()
+        layer.regroup(pair, og_here, s["og"])
+        gain2 = lax.fori_loop(
+            2 * pair, 2 * pair + 2, lambda g, c: layer.feed_forward(s, w, g, c), gain2
+        )
     layer.wide_parts(s, wide_ref)
     wide.start()
-    first = max(1, layer.groups // 4)
-    back = functools.partial(layer.attention_back, s, w)
-    gain1 = lax.fori_loop(0, first, back, zero)
-    wide.to_chips()
-    gain1 = lax.fori_loop(first, layer.groups, back, gain1)
+    for g in range(layer.groups):
+        gain1 = layer.attention_back(s, w, g, gain1)
+        if g == 0:
+            wide.to_chips()
+        if g % 2 == 1:
+            layer.ungroup(g // 2, s["gh"], x_here)
+            y_moves[g // 2].start(x_here, y_ref, y_sems, local.at[2], False)
     layer.square_parts(s, square_ref)
     square.start()
     gains.value[0] = jnp.zeros_like(gains.value[0])
     gains.value[0, 0:1, :] = gain1
     gains.value[0, 1:2, :] = gain2
     gains.start(0)
-    layer.ungroup(s["gh"], x_here)
     wide.to_spaces()
     square.to_chips()
-    y_move.start(x_here, y_ref, y_sems, local.at[2], False)
     gains.value[1] = gains.finish(0)
     gains.start(1)
     wide.gather_spaces()
+    wide.gather_chips()
     square.to_spaces()
     gains.value[2] = gains.finish(1)
     gains.start(2)
-    wide.gather_chips()
     square.gather_spaces()
     wide.gather_cores()
     square.gather_chips()
     gains_out[...] = gains.finish(2) * scale
     square.gather_cores()
-    y_move.wait()
+    for move in y_moves:
+        move.wait()
     wide.wait()
     square.wait()
 
@@ -522,12 +532,12 @@
         scratch_shapes=[
             *scratch.values(),
             *[pltpu.VMEM((everyone, spread, width), BF16)] * 2,
-            *[pltpu.SemaphoreType.DMA((2, groups))] * 3,
-            pltpu.SemaphoreType.DMA((3,)),
+            *[pltpu.SemaphoreType.DMA((spread // 16, 2, groups))] * 3,
+            pltpu.SemaphoreType.DMA((3, spread // 16)),
             pltpu.VMEM((wide_rows, width), F32),
             pltpu.VMEM((square_rows, width), F32),
-            *Total.scratch(wide_rows, width, chips, spaces, BF16),
-            *Total.scratch(square_rows, width, chips, spaces, F32),
+            *Total.scratch(wide_rows, width, chips, spaces),
+            *Total.scratch(square_rows, width, chips, spaces),
             *Gains.scratch(width, chips, spaces),
         ],
         compiler_params=pltpu.CompilerParams(

time: 80.5 us -> 79.5 us (0.988)
  Pallas kernels: 72.8 us -> 71.8 us
    pallas_call x1, Pallas kernels: 72.8 us -> 71.8 us  [on_device(): pl.pallas_call(functools.partial(kernel, layer, scale, tuple(scratch)), o...]
where the time goes in v4:
time: 79.5 us; the launch traced here: 79.3 us
  Pallas kernels  71.8 us (90%)
  local copies, waits for them, and re-layouts  5.76 us (7%)
  other arithmetic  1.08 us (1%)
    pallas_call x1, Pallas kernels, on_device(): pl.pallas_call(functools.partial(kernel, layer, scale, tuple(scratch)), o...  71.8 us
    slice x2, local copies, waits for them, and re-layouts, finish(): return (input_grad, *squares, up, wide[:hidden], gains[0], gains[1])  2.47 us
    slice x1, local copies, waits for them, and re-layouts, finish(): squares = [square[width * i:width * (i + 1)] for i in range(4)]  2.16 us

profile of v4, /device:TPU:0, one launch (start us, length us, event | category | flops | bytes accessed | tf_op | source)
XLA Modules:
  0.0 79.3 jit_solution(18133880794209030246)
XLA Ops:
  0.6 71.8 %shard_map.169 = (bf16[4,256,256]{2,1,0:T(8,128)(2,1)}, bf16[2048,256]{1,0:T(8,128)(2,1)}, bf16[1024,256]{1,0:T(8,128)(2,1)}, f32[8,256]{1,0:T(8,128)}) custom-call(bf16[4,256,256]{2,1,0:T(8,128)(2,1)} %refs_0_.1, bf16[4,256,256]{2,1,0:T(8,128)(2,1)} %refs_1_.1, f32[1,256]{1,0:T(1,128)} %bitcast.11, bf16[256,256]{1,0:T(8,128)(2,1)} %refs_3_.1, ...), custom_call_target="tpu_custom_call" | custom-call | tf_op jit(solution)/shard_map/pallas_call | solution.py:522
  72.5 0.0 copy-start
  72.5 2.2 %fusion.1 = (f32[256,256]{1,0:T(8,128)}, f32[256,256]{1,0:T(8,128)}, f32[256,256]{1,0:T(8,128)}, f32[256,256]{1,0:T(8,128)}) fusion(bf16[1024,256]{1,0:T(8,128)(2,1)} %get-tuple-element.14), kind=kLoop, calls=%fused_computation.2 | loop fusion | bytes 2097152 | tf_op jit(solution)/shard_map/slice | solution.py:555
  74.6 0.0 copy-done
  74.6 1.1 %fusion = (f32[1024,256]{1,0:T(8,128)}, f32[1024,256]{1,0:T(8,128)S(1)}) fusion(bf16[2048,256]{1,0:T(8,128)(2,1)S(1)} %copy-done), kind=kLoop, calls=%fused_computation.1 | loop fusion | bytes 4194304 | tf_op jit(solution)/shard_map/slice | solution.py:556
  75.8 0.0 copy-start.1
  75.8 0.0 copy-start.2
  75.8 1.1 %copy.20 = f32[4,32,8,256]{3,2,0,1:T(8,128)} copy(f32[4,32,8,256]{3,2,1,0:T(8,128)S(1)} %bitcast.9) | data formatting | bytes 2097152 | tf_op jit(solution)/shard_map/reshape | solution.py:554
  76.9 1.3 %fusion.2 = (f32[1,256]{1,0:T(1,128)}, f32[1,256]{1,0:T(1,128)}) fusion(f32[8,256]{1,0:T(8,128)} %get-tuple-element.16), kind=kLoop, calls=%fused_computation.3 | loop fusion | bytes 4096 | tf_op jit(solution)/shard_map/slice | solution.py:556
  78.2 0.0 copy-done.1
  78.2 0.0 copy-done.2
  78.2 1.1 %convert_add_fusion = f32[4,256,256]{2,1,0:T(8,128)} fusion(bf16[4,256,256]{2,1,0:T(8,128)(2,1)S(1)} %copy-done.2, bf16[4,256,256]{2,1,0:T(8,128)(2,1)S(1)} %copy-done.1), kind=kLoop, calls=%fused_computation | loop fusion | flops 786432 | bytes 2097152 | tf_op jit(solution)/shard_map/add | solution.py:551
Async XLA Ops:
  72.5 2.2 %copy-start = (bf16[2048,256]{1,0:T(8,128)(2,1)S(1)}, bf16[2048,256]{1,0:T(8,128)(2,1)}, u32[]{:S(2)}) copy-start(bf16[2048,256]{1,0:T(8,128)(2,1)} %get-tuple-element.15) | copy-start | bytes 3145732
  75.8 2.5 %copy-start.1 = (bf16[4,256,256]{2,1,0:T(8,128)(2,1)S(1)}, bf16[4,256,256]{2,1,0:T(8,128)(2,1)}, u32[]{:S(2)}) copy-start(bf16[4,256,256]{2,1,0:T(8,128)(2,1)} %refs_1_.1) | copy-start | bytes 1572868
  75.8 2.5 %copy-start.2 = (bf16[4,256,256]{2,1,0:T(8,128)(2,1)S(1)}, bf16[4,256,256]{2,1,0:T(8,128)(2,1)}, u32[]{:S(2)}) copy-start(bf16[4,256,256]{2,1,0:T(8,128)(2,1)} %get-tuple-element.13) | copy-start | bytes 1572868
